TPU v7x, 32 devices: a whole 2x2x4 slice. The times are simulated.
32 devices in a mesh: batch: 8 (over z, y), pass: 4 (over x, core).
Axes of the slice: x: 2, y: 2, z: 4, core: 2. Of those that a mesh axis runs over, the one named last changes fastest.
Arguments:
- features: bfloat16 [8192, 4, 4, 256], P(('batch', 'pass')), may hold values from -6 to 6
- labels: int32 [8192, 40], P(('batch', 'pass')), may hold values 0 or 1
- image_counts: int32 [8, 4], P('batch', 'pass'), may hold values from 1 to 256, as said below
- block_one_master: float32 [7168, 512], P(('batch', 'pass')), may hold values from -0.125 to 0.125
- block_one_momentum: float32 [7168, 512], P(('batch', 'pass')), may hold values from -0.00036621094 to 0.00036621094
- block_one_average: float32 [7168, 512], P(('batch', 'pass')), may hold values from -0.125 to 0.125
- block_two_master: float32 [9216, 512], P(('batch', 'pass')), may hold values from -0.09375 to 0.09375
- block_two_momentum: float32 [9216, 512], P(('batch', 'pass')), may hold values from -0.00036621094 to 0.00036621094
- block_two_average: float32 [9216, 512], P(('batch', 'pass')), may hold values from -0.09375 to 0.09375
- norm_params: float32 [2, 5, 512], replicated, may hold values from -0.6 to 1.5, as said below
- norm_momentum: float32 [2, 5, 512], replicated, may hold values from -0.00030517578 to 0.00030517578
- norm_average: float32 [2, 5, 512], replicated, may hold values from -0.6 to 1.5, as said below
- head_params: float32 [513, 40], replicated, may hold values from -0.25 to 0.25
- head_momentum: float32 [513, 40], replicated, may hold values from -0.0625 to 0.0625
- head_average: float32 [513, 40], replicated, may hold values from -0.25 to 0.25
Outputs:
- pooled: float32 [8192, 512], P(('batch', 'pass'))
- input_grad: float32 [8192, 4, 4, 256], P(('batch', 'pass'))
- task_losses: float32 [40], replicated
- task_weights: float32 [40], replicated
- block_one_moment: float32 [7168, 512], P(('batch', 'pass'))
- block_one_weight: float32 [7168, 512], P(('batch', 'pass'))
- block_one_mean: float32 [7168, 512], P(('batch', 'pass'))
- block_one_copy: bfloat16 [7168, 512], P(('batch', 'pass'))
- block_two_moment: float32 [9216, 512], P(('batch', 'pass'))
- block_two_weight: float32 [9216, 512], P(('batch', 'pass'))
- block_two_mean: float32 [9216, 512], P(('batch', 'pass'))
- block_two_copy: bfloat16 [9216, 512], P(('batch', 'pass'))
- norm_moment: float32 [2, 5, 512], replicated
- norm_weight: float32 [2, 5, 512], replicated
- norm_mean: float32 [2, 5, 512], replicated
- head_moment: float32 [513, 40], replicated
- head_weight: float32 [513, 40], replicated
- head_mean: float32 [513, 40], replicated
Inputs may be any that keep to these rules, and one draw needn't show every extreme that they name: image_counts[b, p] is the number of valid images among the 256 slots of device (b, p); they are its first slots, the rest are padding. Some device has all 256 slots valid. norm_params[0] holds gains, norm_params[1] shifts. norm_average[0] holds gains, norm_average[1] shifts.
All inputs are finite; a program needn't handle non-finite values. No bound on the sum of `labels` on one device may be relied on, other than what follows from the above.
Results may differ from a plain program's by a relative error of at most 0.012.
Values may be sent and summed in bfloat16 or wider, within the bound.
No kernel may reach another device: no remote copies, remote signals or barrier semaphores. Data moves between devices by JAX's collectives and lax.ppermute only.
A program may use at most 320 MiB of HBM per device.

v0:
```python
import math

import jax
import jax.numpy as jnp
import numpy as np
from jax import lax
from jax.sharding import PartitionSpec as P

CIN = 256
COUT = 512
TASKS = 40
FW_STEPS = 20
CAP = 256


epsilon = 1e-05
softness = 0.01
momentum_decay = 0.9
average_decay = 0.9
rate_conv = 3.0
rate_norm = 50.0
rate_head = 0.05
highest = lax.Precision.HIGHEST


def silu_value(v):
    return v * jax.nn.sigmoid(v)


def silu_slope(v):
    sigma = jax.nn.sigmoid(v)
    return sigma * (1.0 + v * (1.0 - sigma))


def matmul(left, right):
    return jnp.dot(left, right, preferred_element_type=jnp.float32)


def matmul_right_t(left, right):
    return lax.dot_general(
        left, right, (((1,), (1,)), ((), ())), preferred_element_type=jnp.float32
    )


def matmul_left_t(left, right):
    return lax.dot_general(
        left, right, (((0,), (0,)), ((), ())), preferred_element_type=jnp.float32
    )


def tap_table(side_in, stride):
    table = np.zeros((side_in * side_in, 4, 9), np.float32)
    for row_in in range(side_in):
        for col_in in range(side_in):
            for row_out in range(2):
                for col_out in range(2):
                    row_tap = row_in - stride * row_out + 1
                    col_tap = col_in - stride * col_out + 1
                    if 0 <= row_tap < 3 and 0 <= col_tap < 3:
                        table[
                            row_in * side_in + col_in, row_out * 2 + col_out, row_tap * 3 + col_tap
                        ] = 1.0
    return table


def short_table():
    table = np.zeros((16, 4, 1), np.float32)
    for row_out in range(2):
        for col_out in range(2):
            table[2 * row_out * 4 + 2 * col_out, row_out * 2 + col_out, 0] = 1.0
    return table


def spread_weight(table, weight, channels):
    cells_in, cells_out, taps = table.shape
    stacked = weight.reshape(taps, channels, weight.shape[1])
    dense = jnp.einsum(
        "iot,tcd->icod",
        jnp.asarray(table, jnp.bfloat16),
        stacked,
        preferred_element_type=jnp.float32,
    )
    return dense.astype(jnp.bfloat16).reshape(cells_in * channels, cells_out * weight.shape[1])


def collect_weight_grad(table, left_flat, grad_flat, channels):
    cells_in, cells_out, taps = table.shape
    dense = matmul_left_t(left_flat, grad_flat)
    dense = dense.reshape(cells_in, channels, cells_out, dense.shape[1] // cells_out)
    folded = jnp.einsum("iot,icod->tcd", jnp.asarray(table, jnp.float32), dense, precision=highest)
    return folded.reshape(taps * channels, folded.shape[2])


def standardize(values, mask_rows, slot_positions):
    first_part = jnp.stack([jnp.sum(v * mask_rows, axis=0) for v in values])
    square_part = jnp.stack([jnp.sum(mask_rows * v * v, axis=0) for v in values])
    first_sum, second_sum = lax.psum((first_part, square_part), ("batch", "pass"))
    centre = first_sum / slot_positions
    spread = second_sum / slot_positions - centre * centre
    inverse_spread = lax.rsqrt(spread + epsilon)
    return ([(v - centre[k]) * inverse_spread[k] for k, v in enumerate(values)], inverse_spread)


def norm_reverse(incoming, standardized, inverse_spread, row_scales, mask_rows, slot_positions):
    partial_scale = jnp.stack(
        [jnp.sum(mask_rows * g * s, axis=0) for g, s in zip(incoming, standardized)]
    )
    shift_part = jnp.stack([jnp.sum(mask_rows * g, axis=0) for g in incoming])
    scale_total, shift_total = lax.psum((partial_scale, shift_part), ("batch", "pass"))
    outputs = []
    for k in range(len(incoming)):
        inner_product = (
            incoming[k]
            - mask_rows * (shift_total[k] + standardized[k] * scale_total[k]) / slot_positions
        )
        outputs.append(row_scales[k] * inverse_spread[k] * inner_product)
    return (scale_total, shift_total, outputs)


def reduce_rows(full_grad):
    return lax.psum_scatter(full_grad, ("batch", "pass"), scatter_dimension=0, tiled=True)


def frank_wolfe(gram):
    scaled = gram / (jnp.mean(jnp.diagonal(gram)) + 1e-06)
    weights = jnp.full((TASKS,), 1.0 / TASKS, jnp.float32)
    for turn in range(FW_STEPS):
        activation_slope = jnp.dot(scaled, weights, precision=highest)
        target_labels = jax.nn.softmax(-activation_slope / softness)
        gamma = 2.0 / (turn + 3.0)
        weights = (1.0 - gamma) * weights + gamma * target_labels
    return weights


def nesterov(grad, master, momentum, average, rate):
    moment = momentum_decay * momentum + grad
    fresh = master - rate * (grad + momentum_decay * moment)
    return (moment, fresh, average_decay * average + (1.0 - average_decay) * fresh)


def shards(
    features,
    labels,
    image_counts,
    block_one_master,
    block_one_momentum,
    block_one_average,
    block_two_master,
    block_two_momentum,
    block_two_average,
    norm_params,
    norm_momentum,
    norm_average,
    head_params,
    head_momentum,
    head_average,
):
    images_all = CAP * lax.axis_size("batch") * lax.axis_size("pass")
    valid_count = image_counts[0, 0]
    valid = (jnp.arange(CAP) < valid_count).astype(jnp.float32)
    mask_rows = jnp.repeat(valid, 4)[:, None]
    row_total = CAP * 4
    total = lax.psum(valid_count.astype(jnp.float32), ("batch", "pass"))
    slot_positions = 4.0 * total
    block_one, block_two = (
        lax.all_gather(
            block_one_master.astype(jnp.bfloat16), ("batch", "pass"), axis=0, tiled=True
        ),
        lax.all_gather(
            block_two_master.astype(jnp.bfloat16), ("batch", "pass"), axis=0, tiled=True
        ),
    )
    scale_factors = norm_params[0]
    start_offsets = norm_params[1]
    stride_taps = tap_table(4, 2)
    plain_taps = tap_table(2, 1)
    short_taps = short_table()
    dense_first = spread_weight(stride_taps, block_one[: 9 * CIN], CIN)
    dense_short = spread_weight(short_taps, block_one[9 * CIN : 10 * CIN], CIN)
    dense_second = spread_weight(plain_taps, block_one[10 * CIN :], COUT)
    dense_third = spread_weight(plain_taps, block_two[: 9 * COUT], COUT)
    dense_fourth = spread_weight(plain_taps, block_two[9 * COUT :], COUT)
    input_flat = features.reshape(CAP, 16 * CIN)
    conv_output_first = matmul(input_flat, dense_first).reshape(row_total, COUT)
    conv_output_shortcut = matmul(input_flat, dense_short).reshape(row_total, COUT)
    pair_std, pair_inverse = standardize(
        [conv_output_first, conv_output_shortcut], mask_rows, slot_positions
    )
    preact_first = scale_factors[0] * pair_std[0] + start_offsets[0]
    a_first_flat = silu_value(preact_first).astype(jnp.bfloat16).reshape(CAP, 4 * COUT)
    conv_output_second = matmul(a_first_flat, dense_second).reshape(row_total, COUT)
    second_std, second_inverse = standardize([conv_output_second], mask_rows, slot_positions)
    preact_one = (
        scale_factors[1] * second_std[0]
        + start_offsets[1]
        + (scale_factors[2] * pair_std[1] + start_offsets[2])
    )
    hidden_first = silu_value(preact_one)
    hidden_flat = hidden_first.astype(jnp.bfloat16).reshape(CAP, 4 * COUT)
    conv_output_third = matmul(hidden_flat, dense_third).reshape(row_total, COUT)
    third_std, third_inverse = standardize([conv_output_third], mask_rows, slot_positions)
    preact_three = scale_factors[3] * third_std[0] + start_offsets[3]
    a_third_flat = silu_value(preact_three).astype(jnp.bfloat16).reshape(CAP, 4 * COUT)
    conv_output_fourth = matmul(a_third_flat, dense_fourth).reshape(row_total, COUT)
    fourth_std, fourth_inverse = standardize([conv_output_fourth], mask_rows, slot_positions)
    preact_two = scale_factors[4] * fourth_std[0] + start_offsets[4] + hidden_first
    h_two = silu_value(preact_two)
    pooled = jnp.mean(h_two.reshape(CAP, 4, COUT), axis=1)
    weight_rows = head_params[:COUT]
    logits = jnp.dot(pooled, weight_rows, precision=highest) + head_params[COUT]
    target_labels = labels.astype(jnp.float32)
    resid = (jax.nn.sigmoid(logits) - target_labels) * valid[:, None]
    loss_part = jnp.sum(valid[:, None] * (jax.nn.softplus(logits) - target_labels * logits), axis=0)
    gram_part = jnp.dot(resid.T, resid, precision=highest)
    lifted = jnp.concatenate([pooled, jnp.ones((CAP, 1), jnp.float32)], axis=1)
    head_part = jnp.dot(lifted.T, resid, precision=highest)
    gram_sum, head_sum, loss_sum = lax.psum((gram_part, head_part, loss_part), ("batch", "pass"))
    task_losses = loss_sum / total
    head_grad = head_sum / total
    gram = gram_sum * jnp.dot(weight_rows.T, weight_rows, precision=highest) / total
    task_weights = frank_wolfe(gram)
    pooled_grad = jnp.dot(resid * task_weights / total, weight_rows.T, precision=highest)
    h_two_grad = jnp.broadcast_to(pooled_grad[:, None, :] / 4.0, (CAP, 4, COUT)).reshape(
        row_total, COUT
    )
    preact_two_gradient = h_two_grad * silu_slope(preact_two)
    scale_four, shift_four, dy_list = norm_reverse(
        [preact_two_gradient],
        fourth_std,
        fourth_inverse,
        scale_factors[4:5],
        mask_rows,
        slot_positions,
    )
    dy_fourth = dy_list[0].astype(jnp.bfloat16).reshape(CAP, 4 * COUT)
    w_fourth_grad = collect_weight_grad(plain_taps, a_third_flat, dy_fourth, COUT)
    a_third_grad = matmul_right_t(dy_fourth, dense_fourth).reshape(row_total, COUT)
    preact_three_gradient = a_third_grad * silu_slope(preact_three)
    scale_three, shift_three, dy_list = norm_reverse(
        [preact_three_gradient],
        third_std,
        third_inverse,
        scale_factors[3:4],
        mask_rows,
        slot_positions,
    )
    dy_third = dy_list[0].astype(jnp.bfloat16).reshape(CAP, 4 * COUT)
    w_third_grad = collect_weight_grad(plain_taps, hidden_flat, dy_third, COUT)
    block_two_grad = jnp.concatenate([w_third_grad, w_fourth_grad], axis=0)
    block_two_sum = reduce_rows(block_two_grad)
    h_one_grad = preact_two_gradient + matmul_right_t(dy_third, dense_third).reshape(
        row_total, COUT
    )
    u_one_grad = h_one_grad * silu_slope(preact_one)
    scale_pair, shift_pair, dy_list = norm_reverse(
        [u_one_grad, u_one_grad],
        [second_std[0], pair_std[1]],
        jnp.stack([second_inverse[0], pair_inverse[1]]),
        scale_factors[1:3],
        mask_rows,
        slot_positions,
    )
    dy_second = dy_list[0].astype(jnp.bfloat16).reshape(CAP, 4 * COUT)
    dy_short = dy_list[1].astype(jnp.bfloat16).reshape(CAP, 4 * COUT)
    w_second_grad = collect_weight_grad(plain_taps, a_first_flat, dy_second, COUT)
    a_first_grad = matmul_right_t(dy_second, dense_second).reshape(row_total, COUT)
    preact_first_gradient = a_first_grad * silu_slope(preact_first)
    scale_first, shift_first, dy_list = norm_reverse(
        [preact_first_gradient],
        pair_std[0:1],
        pair_inverse[0:1],
        scale_factors[0:1],
        mask_rows,
        slot_positions,
    )
    dy_first = dy_list[0].astype(jnp.bfloat16).reshape(CAP, 4 * COUT)
    w_first_grad = collect_weight_grad(stride_taps, input_flat, dy_first, CIN)
    w_short_grad = collect_weight_grad(short_taps, input_flat, dy_short, CIN)
    block_one_grad = jnp.concatenate([w_first_grad, w_short_grad, w_second_grad], axis=0)
    block_one_sum = reduce_rows(block_one_grad)
    input_grad = (
        matmul_right_t(dy_first, dense_first) + matmul_right_t(dy_short, dense_short)
    ).reshape(CAP, 4, 4, CIN)
    scale_grads = jnp.stack(
        [scale_first[0], scale_pair[0], scale_pair[1], scale_three[0], scale_four[0]]
    )
    shift_grads = jnp.stack(
        [shift_first[0], shift_pair[0], shift_pair[1], shift_three[0], shift_four[0]]
    )
    norm_grad = jnp.stack([scale_grads, shift_grads])
    scale_rate = math.sqrt(images_all)
    one_m, one_w, one_a = nesterov(
        block_one_sum,
        block_one_master,
        block_one_momentum,
        block_one_average,
        rate_conv * scale_rate,
    )
    two_m, two_w, two_a = nesterov(
        block_two_sum,
        block_two_master,
        block_two_momentum,
        block_two_average,
        rate_conv * scale_rate,
    )
    norm_m, norm_w, norm_a = nesterov(
        norm_grad, norm_params, norm_momentum, norm_average, rate_norm * scale_rate
    )
    head_m, head_w, head_a = nesterov(
        head_grad, head_params, head_momentum, head_average, rate_head * scale_rate
    )
    return (
        pooled,
        input_grad,
        task_losses,
        task_weights,
        one_m,
        one_w,
        one_a,
        one_w.astype(jnp.bfloat16),
        two_m,
        two_w,
        two_a,
        two_w.astype(jnp.bfloat16),
        norm_m,
        norm_w,
        norm_a,
        head_m,
        head_w,
        head_a,
    )


def solution(mesh):
    in_specs = (
        P(("batch", "pass"), None, None, None),
        P(("batch", "pass"), None),
        P("batch", "pass"),
        P(("batch", "pass"), None),
        P(("batch", "pass"), None),
        P(("batch", "pass"), None),
        P(("batch", "pass"), None),
        P(("batch", "pass"), None),
        P(("batch", "pass"), None),
        P(),
        P(),
        P(),
        P(),
        P(),
        P(),
    )
    out_specs = (
        P(("batch", "pass"), None),
        P(("batch", "pass"), None, None, None),
        P(),
        P(),
        P(("batch", "pass"), None),
        P(("batch", "pass"), None),
        P(("batch", "pass"), None),
        P(("batch", "pass"), None),
        P(("batch", "pass"), None),
        P(("batch", "pass"), None),
        P(("batch", "pass"), None),
        P(("batch", "pass"), None),
        P(),
        P(),
        P(),
        P(),
        P(),
        P(),
    )
    return jax.shard_map(shards, mesh=mesh, in_specs=in_specs, out_specs=out_specs, check_vma=False)
```

profile of v0, /device:TPU:0, one launch (start us, length us, event | category | flops | bytes accessed | tf_op | source)
XLA Modules:
  0.0 1397.6 jit_solution(16622168601023024027)
XLA Ops:
  15.5 72.2 %all-gather.3.cloned.1.call-done = bf16[7168,512]{1,0:T(8,128)(2,1)} async-done(((bf16[224,512]{1,0:T(8,128)(2,1)}), bf16[7168,512]{1,0:T(8,128)(2,1)}) %all-gather.3.cloned.1.call-update) | async-done | bytes 7340048 | tf_op jit(solution)/shard_map/all_gather | solution.py:166
  125.1 30.9 %copy.117 = bf16[16,256,4,512]{1,0,3,2:T(8,128)(2,1)} copy(bf16[16,256,4,512]{3,0,1,2:T(8,128)(2,1)} %convert_bitcast_fusion) | data formatting | bytes 33554432 | tf_op jit(solution)/shard_map/convert_element_type | solution.py:83
  203.9 39.4 %all-reduce.8 = (f32[2,512]{1,0:T(2,128)S(1)}, f32[]{:T(128)}, f32[2,512]{1,0:T(2,128)S(1)}) all-reduce(f32[2,512]{1,0:T(2,128)S(1)} %get-tuple-element.206, f32[]{:T(128)S(6)} %convert_element_type.105, f32[2,512]{1,0:T(2,128)S(1)} %get-tuple-element.207), channel_id=1, replica_groups=mesh['batch'=8,'pass'=4] {'batch','pass'}, use_global_device_ids=true, to_apply=%region_2.0 | all-reduce | flops 2049 | bytes 16392 | tf_op jit(solution)/shard_map/psum | solution.py:97
  260.2 40.5 %all-reduce.7 = (f32[1,512]{1,0:T(1,128)S(1)}, f32[1,512]{1,0:T(1,128)S(1)}) all-reduce(f32[1,512]{1,0:T(1,128)S(1)} %bitcast.854, f32[1,512]{1,0:T(1,128)S(1)} %bitcast.853), channel_id=1, replica_groups=mesh['batch'=8,'pass'=4] {'batch','pass'}, use_global_device_ids=true, to_apply=%region_8.0 | all-reduce | flops 1024 | bytes 8192 | tf_op jit(solution)/shard_map/psum | solution.py:97
  374.7 40.3 %all-reduce.6 = (f32[1,512]{1,0:T(1,128)S(1)}, f32[1,512]{1,0:T(1,128)S(1)}) all-reduce(f32[1,512]{1,0:T(1,128)S(1)} %bitcast.856, f32[1,512]{1,0:T(1,128)S(1)} %bitcast.855), channel_id=1, replica_groups=mesh['batch'=8,'pass'=4] {'batch','pass'}, use_global_device_ids=true, to_apply=%region_12.0 | all-reduce | flops 1024 | bytes 8192 | tf_op jit(solution)/shard_map/psum | solution.py:97
  430.7 39.9 %all-reduce.5 = (f32[1,512]{1,0:T(1,128)S(1)}, f32[1,512]{1,0:T(1,128)S(1)}) all-reduce(f32[1,512]{1,0:T(1,128)S(1)} %bitcast.858, f32[1,512]{1,0:T(1,128)S(1)} %bitcast.857), channel_id=1, replica_groups=mesh['batch'=8,'pass'=4] {'batch','pass'}, use_global_device_ids=true, to_apply=%region_16.0 | all-reduce | flops 1024 | bytes 8192 | tf_op jit(solution)/shard_map/psum | solution.py:97
  477.6 40.3 %psum.149 = f32[40,40]{1,0:T(8,128)S(1)} all-reduce(f32[40,40]{1,0:T(8,128)S(1)} %fusion.204), channel_id=1, replica_groups=mesh['batch'=8,'pass'=4] {'batch','pass'}, use_global_device_ids=true, to_apply=%region_20.21 | all-reduce | flops 1600 | bytes 12800 | tf_op jit(solution)/shard_map/psum | solution.py:217
  598.7 40.2 %all-reduce.4 = (f32[1,512]{1,0:T(1,128)S(1)}, f32[1,512]{1,0:T(1,128)S(1)}) all-reduce(f32[1,512]{1,0:T(1,128)S(1)} %bitcast.846, f32[1,512]{1,0:T(1,128)S(1)} %bitcast.845), channel_id=1, replica_groups=mesh['batch'=8,'pass'=4] {'batch','pass'}, use_global_device_ids=true, to_apply=%region_67.68 | all-reduce | flops 1024 | bytes 8192 | tf_op jit(solution)/shard_map/psum | solution.py:109
  661.1 40.1 %all-reduce.3 = (f32[1,512]{1,0:T(1,128)S(1)}, f32[1,512]{1,0:T(1,128)S(1)}) all-reduce(f32[1,512]{1,0:T(1,128)S(1)} %bitcast.835, f32[1,512]{1,0:T(1,128)S(1)} %bitcast.834), channel_id=1, replica_groups=mesh['batch'=8,'pass'=4] {'batch','pass'}, use_global_device_ids=true, to_apply=%region_71.72 | all-reduce | flops 1024 | bytes 8192 | tf_op jit(solution)/shard_map/psum | solution.py:109
  710.0 33.9 %fusion.12 = f32[9,512,512]{2,0,1:T(8,128)} fusion(f32[4,4,9,1]{2,1,0,3:T(4,128)S(1)} %copy-done.33, f32[4,512,4,512]{3,1,2,0:T(8,128)S(1)} %fusion.210), kind=kOutput, calls=%fused_computation.13 | convolution fusion | flops 452984832 | bytes 26214976 | tf_op jit(solution)/shard_map/iot,icod->tcd/dot_general | solution.py:90
  762.7 33.8 %fusion.9 = f32[9,512,512]{2,0,1:T(8,128)} fusion(f32[4,4,9,1]{2,1,0,3:T(4,128)S(1)} %copy-done.33, f32[4,512,4,512]{3,1,2,0:T(8,128)S(1)} %fusion.209), kind=kOutput, calls=%fused_computation.12 | convolution fusion | flops 452984832 | bytes 26214976 | tf_op jit(solution)/shard_map/iot,icod->tcd/dot_general | solution.py:90
  811.4 17.3 %pad_maximum_fusion = f32[9216,512]{1,0:T(8,128)} fusion(f32[4608,512]{1,0:T(8,128)} %bitcast.641, f32[4608,512]{1,0:T(8,128)} %bitcast.642), kind=kLoop, calls=%fused_computation.2 | loop fusion | flops 4718592 | bytes 37748736 | tf_op jit(solution)/shard_map/concatenate | solution.py:249
  861.4 40.9 %all-reduce.2 = (f32[2,512]{1,0:T(2,128)S(1)}, f32[2,512]{1,0:T(2,128)S(1)}) all-reduce(f32[2,512]{1,0:T(2,128)S(1)} %pad_maximum_fusion.6, f32[2,512]{1,0:T(2,128)S(1)} %pad_maximum_fusion.5), channel_id=1, replica_groups=mesh['batch'=8,'pass'=4] {'batch','pass'}, use_global_device_ids=true, to_apply=%region_76.77 | all-reduce | flops 2048 | bytes 16384 | tf_op jit(solution)/shard_map/psum | solution.py:109
  927.9 39.9 %all-reduce.1 = (f32[1,512]{1,0:T(1,128)S(1)}, f32[1,512]{1,0:T(1,128)S(1)}, f32[40]{0:T(128)}) all-reduce(f32[1,512]{1,0:T(1,128)S(1)} %bitcast.833, f32[1,512]{1,0:T(1,128)S(1)} %bitcast.832, f32[40]{0:T(128)S(1)} %get-tuple-element.138), channel_id=1, replica_groups=mesh['batch'=8,'pass'=4] {'batch','pass'}, use_global_device_ids=true, to_apply=%region_80.81 | all-reduce | flops 1064 | bytes 8512 | tf_op jit(solution)/shard_map/psum | solution.py:109
  971.6 34.0 %fusion.6 = f32[9,512,512]{2,0,1:T(8,128)} fusion(f32[4,4,9,1]{2,1,0,3:T(4,128)S(1)} %copy-done.33, f32[4,512,4,512]{3,1,2,0:T(8,128)S(1)} %fusion.208), kind=kOutput, calls=%fused_computation.11 | convolution fusion | flops 452984832 | bytes 26214976 | tf_op jit(solution)/shard_map/iot,icod->tcd/dot_general | solution.py:90
  1020.5 16.4 %fusion.170 = f32[2048,4096]{1,0:T(8,128)} fusion(bf16[256,4096]{1,0:T(8,128)(2,1)} %reshape.558, f32[2048]{0:T(1024)S(1)} %bitcast.738, f32[2048]{0:T(1024)S(1)} %bitcast.736, f32[2048]{0:T(1024)S(1)} %bitcast.734, f32[]{:T(128)S(6)} %mul.1158, f32[256]{0:T(256)S(1)} %compare_convert_fusion, f32[2048]{0:T(1024)S(1)} %bitcast.698, f32[2048]{0:T(1024)S(1)} %bitcast.704, ...), kind=kOutput, calls=%fused_computation.362 | convolution fusion | flops 4308074496 | bytes 44131332 | tf_op jit(solution)/shard_map/dot_general | solution.py:46
  1036.9 30.2 %copy.204 = f32[256,8,16,256]{3,2,1,0:T(8,128)} copy(f32[256,8,16,256]{3,1,2,0:T(8,128)} %bitcast.632) | data formatting | bytes 67108864
  1067.1 21.1 %fusion.207 = f32[1,256,512,1]{1,0,2,3:T(1,128)S(1)} fusion(f32[16,256,4,512]{1,0,3,2:T(8,128)} %bitcast.633, f32[16,4,1,1]{0,2,3,1:T(1,128)S(1)} %copy-done.68), kind=kOutput, calls=%fused_computation.399 | convolution fusion | flops 100663296 | bytes 34078976 | tf_op jit(solution)/shard_map/iot,icod->tcd/dot_general | solution.py:90
  1088.8 16.1 %fusion.168 = f32[2048,4096]{1,0:T(8,128)} fusion(bf16[256,4096]{1,0:T(8,128)(2,1)} %reshape.558, f32[256,2048]{0,1:T(8,128)} %copy.133, f32[2048]{0:T(1024)S(1)} %bitcast.744, f32[2048]{0:T(1024)S(1)} %bitcast.742, f32[]{:T(128)S(6)} %mul.1158, f32[256]{0:T(256)S(1)} %compare_convert_fusion, f32[2048]{0:T(1024)S(1)} %bitcast.740, f32[2048]{0:T(1024)S(1)} %bitcast.720, ...), kind=kOutput, calls=%fused_computation.360 | convolution fusion | flops 4304928768 | bytes 39904260 | tf_op jit(solution)/shard_map/dot_general | solution.py:46
  1104.9 30.2 %copy.203 = f32[256,8,16,256]{3,2,1,0:T(8,128)} copy(f32[256,8,16,256]{3,1,2,0:T(8,128)} %bitcast.631) | data formatting | bytes 67108864
  1135.1 39.8 %copy.134 = f32[16,256,4,512]{3,0,2,1:T(8,128)} copy(f32[16,256,4,512]{1,0,3,2:T(8,128)} %bitcast.634) | data formatting | bytes 67108864 | tf_op jit(solution)/shard_map/reshape | solution.py:89
  1174.8 37.5 %convolution_bitcast_fusion = f32[9,256,512]{2,0,1:T(8,128)S(1)} fusion(f32[16,4,9,1]{0,2,1,3:T(8,128)S(1)} %copy-done.36, f32[16,256,4,512]{3,0,2,1:T(8,128)} %copy.134), kind=kOutput, calls=%fused_computation.29 | convolution fusion | flops 905969664 | bytes 38275328 | tf_op jit(solution)/shard_map/iot,icod->tcd/dot_general | solution.py:90
  1238.9 16.2 %convolution_add_fusion = f32[256,4096]{1,0:T(8,128)} fusion(f32[256,4096]{1,0:T(8,128)S(1)} %fusion.169, bf16[4096,2048]{0,1:T(8,128)(2,1)} %bitcast.654, f32[2048]{0:T(1024)S(1)} %bitcast.739, f32[2048]{0:T(1024)S(1)} %bitcast.737, f32[2048]{0:T(1024)S(1)} %bitcast.735, f32[]{:T(128)S(6)} %mul.1158, f32[256]{0:T(256)S(1)} %compare_convert_fusion, ...), kind=kOutput, calls=%fused_computation.26 | convolution fusion | flops 4309123072 | bytes 33645572 | tf_op jit(solution)/shard_map/dot_general | solution.py:40
  1270.2 117.5 %reduce-scatter.3.cloned.1.call-done = f32[224,512]{1,0:T(8,128)} async-done(((f32[7168,512]{1,0:T(8,128)}), f32[224,512]{1,0:T(8,128)}) %reduce-scatter.3.cloned.1.call-update) | async-done | bytes 458768 | tf_op jit(solution)/shard_map/reduce_scatter | solution.py:121
  (400 shorter events, 470.8 us)
Async XLA Ops:
  7.2 80.5 %all-gather.3.cloned.1.call-start = ((), (), s32[]{:S(2)}) async-start(), calls=%async_computation.2 | async-start | bytes 7569408 | tf_op jit(solution)/shard_map/all_gather | solution.py:166
  9.2 297.5 %all-gather.5.cloned.1.call-start = ((), (), s32[]{:S(2)}) async-start(), calls=%async_computation.3 | async-start | bytes 9732096 | tf_op jit(solution)/shard_map/all_gather | solution.py:169
  11.0 1253.6 %all-reduce.11.cloned.1.call-start = ((), (), s32[]{:S(2)}) async-start(), calls=%async_computation.6 | async-start | bytes 204800 | tf_op jit(solution)/shard_map/psum | solution.py:217
  156.0 11.9 copy-start.7
  200.9 44.3 %copy-start.5 = (f32[2048,256]{1,0:T(8,128)S(1)}, f32[2048,256]{1,0:T(8,128)}, u32[]{:S(2)}) copy-start(f32[2048,256]{1,0:T(8,128)} %copy-done.4) | copy-start | bytes 6291460
  325.5 10.4 copy-start.1
  363.9 10.4 copy-start.9
  657.6 609.3 %reduce-scatter.5.cloned.1.call-start = ((), (), s32[]{:S(2)}) async-start(), calls=%async_computation.5 | async-start | bytes 19464192 | tf_op jit(solution)/shard_map/reduce_scatter | solution.py:121
  828.7 558.9 %reduce-scatter.3.cloned.1.call-start = ((), (), s32[]{:S(2)}) async-start(), calls=%async_computation.4 | async-start | bytes 15138816 | tf_op jit(solution)/shard_map/reduce_scatter | solution.py:121
  924.4 43.5 %copy-start.14 = (bf16[2048,256]{1,0:T(8,128)(2,1)S(1)}, bf16[2048,256]{1,0:T(8,128)(2,1)}, u32[]{:S(2)}) copy-start(bf16[2048,256]{1,0:T(8,128)(2,1)} %multiply_convert_fusion.2) | copy-start | bytes 3145732
  1036.9 30.2 %copy-start.68 = (f32[16,4,1,1]{0,2,3,1:T(1,128)S(1)}, f32[16,4,1,1]{0,2,3,1:T(1,128)}, u32[]{:S(2)}) copy-start(f32[16,4,1,1]{0,2,3,1:T(1,128)} %constant.184) | copy-start | bytes 772
  1135.1 39.8 %copy-start.36 = (f32[16,4,9,1]{0,2,1,3:T(8,128)S(1)}, f32[16,4,9,1]{0,2,1,3:T(8,128)}, u32[]{:S(2)}) copy-start(f32[16,4,9,1]{0,2,1,3:T(8,128)} %constant.183) | copy-start | bytes 6916
  1225.2 13.6 copy-start.2
  1225.3 13.6 copy-start.3
  1225.3 13.6 copy-start.6
  1255.1 9.5 copy-start.24
  1255.2 9.5 copy-start.31
  1255.2 9.5 copy-start.32
  1255.2 11.8 copy-start.19
  1255.2 11.8 copy-start.25
  1266.9 120.7 %copy-start.21 = (f32[224,512]{1,0:T(8,128)S(1)}, f32[224,512]{1,0:T(8,128)}, u32[]{:S(2)}) copy-start(f32[224,512]{1,0:T(8,128)} %param.28) | copy-start | bytes 1376260
  1266.9 120.7 %copy-start.27 = (f32[224,512]{1,0:T(8,128)S(1)}, f32[224,512]{1,0:T(8,128)}, u32[]{:S(2)}) copy-start(f32[224,512]{1,0:T(8,128)} %param.29) | copy-start | bytes 1376260
  1269.2 120.5 %copy-start.18 = (f32[288,512]{1,0:T(8,128)}, f32[288,512]{1,0:T(8,128)S(1)}, u32[]{:S(2)}) copy-start(f32[288,512]{1,0:T(8,128)S(1)} %get-tuple-element.117) | copy-start | bytes 1769476
  1269.2 120.5 %copy-start.28 = (f32[224,512]{1,0:T(8,128)S(1)}, f32[224,512]{1,0:T(8,128)}, u32[]{:S(2)}) copy-start(f32[224,512]{1,0:T(8,128)} %param.30) | copy-start | bytes 1376260
  (54 other events, 206.5 us)
Sparse Core Ops, SparseCore 0:
  11.5 76.1 all-gather.2
  91.2 80.5 all-gather.4
  657.8 120.2 all-reduce.10
  828.9 207.0 reduce-scatter.4
  1225.4 162.2 reduce-scatter.2
where the time goes:
time: 1410 us; the launch traced here: 1400 us
  blocking collectives  361 us (26%)
  matrix products  356 us (25%)
  local copies, waits for them, and re-layouts  313 us (22%)
  waiting for transfers between devices  190 us (13%)
  other arithmetic  159 us (11%)
  between operations  18.3 us (1%)
    psum x4, blocking collectives, norm_reverse(): lax.psum((partial_scale, shift_part), ('batch', 'pass'))  161 us
    dot_general x5, matrix products, collect_weight_grad(): jnp.einsum('iot,icod->tcd', jnp.asarray(table, jnp.float32), dense, preci...  160 us
    psum x4, blocking collectives, standardize(): lax.psum((first_part, square_part), ('batch', 'pass'))  160 us
    unnamed x225, local copies, waits for them, and re-layouts  120 us
    reduce_scatter x2, waiting for transfers between devices, reduce_rows(): lax.psum_scatter(full_grad, ('batch', 'pass'), scatter_dimension=0, tiled...  117 us
    all_gather x1, waiting for transfers between devices, shards(): lax.all_gather(block_one_master.astype(jnp.bfloat16), ('batch', 'pass'),...  72.2 us
    dot_general x5, matrix products, matmul_right_t(): lax.dot_general(left, right, (((1,), (1,)), ((), ())), preferred_element_...  54.7 us
    dot_general x5, local copies, waits for them, and re-layouts, collect_weight_grad(): jnp.einsum('iot,icod->tcd', jnp.asarray(table, jnp.float32), dense, preci...  48 us
  transfers between devices with their start and end apart: 5, of which 2 were waited for; matrix products, arithmetic and copies ran while one was open for 45% of the time, Pallas kernels for 0%

commit v1 on v0

v1 whole, which is shorter than its diff:
```python
import math

import jax
import jax.numpy as jnp
from jax import lax
from jax.experimental import pallas as pl
from jax.experimental.pallas import tpu as pltpu
from jax.sharding import PartitionSpec as P

CIN = 256
COUT = 512
TASKS = 40
FW_STEPS = 20
CAP = 256
WIDE = 4 * COUT
LANES = 128
AXES = ("batch", "pass")

epsilon = 1e-05
softness = 0.01
momentum_decay = 0.9
average_decay = 0.9
rate_conv = 3.0
rate_norm = 50.0
rate_head = 0.05
highest = lax.Precision.HIGHEST

HBM = pl.BlockSpec(memory_space=pltpu.HBM)
VMEM = pl.BlockSpec(memory_space=pltpu.VMEM)
SMEM = pl.BlockSpec(memory_space=pltpu.SMEM)
f32 = jnp.float32
bf16 = jnp.bfloat16


def shape(extent, kind):
    return jax.ShapeDtypeStruct(extent, kind)


def run(body, args, in_specs, outs, out_specs, scratch, flops=0, moved=0, aliases=None, name=None):
    return pl.pallas_call(
        body,
        out_shape=outs,
        in_specs=in_specs,
        out_specs=out_specs,
        scratch_shapes=scratch,
        input_output_aliases=aliases or {},
        compiler_params=pltpu.CompilerParams(vmem_limit_bytes=60 * 1024 * 1024),
        cost_estimate=pl.CostEstimate(flops=flops, bytes_accessed=moved, transcendentals=0),
        name=name,
    )(*args)


class Mover:
    def __init__(self, sems):
        self.sems = sems
        self.used = 0
        self.out = []

    def load(self, src, dst):
        copy = pltpu.make_async_copy(src, dst, self.sems.at[self.used])
        self.used += 1
        copy.start()
        return copy

    def store(self, src, dst):
        self.out.append(self.load(src, dst))

    def finish(self):
        for copy in self.out:
            copy.wait()


def columns(o):
    return pl.ds(o * COUT, COUT)


def split_turn(at, tb, value, place, channels):
    half = channels // 2
    tb[pl.ds(0, channels), :] = value.T
    for group in range(half // 16):
        for parity in range(2):
            at[parity, pl.ds(place * half + 16 * group, 16), :] = tb[
                pl.ds(32 * group + 16 * parity, 16), :
            ]


def hand_out(move, at, side_ref, mine_ref, theirs_ref):
    side = side_ref[0, 0]
    move.store(at.at[side], mine_ref)
    move.store(at.at[1 - side], theirs_ref)


def dot(left, right, precision=None):
    return jnp.dot(left, right, preferred_element_type=f32, precision=precision)


def dot_nt(left, right):
    return lax.dot_general(left, right, (((1,), (1,)), ((), ())), preferred_element_type=f32)


def dot_tn(left, right, precision=None):
    return lax.dot_general(
        left, right, (((0,), (0,)), ((), ())), preferred_element_type=f32, precision=precision
    )


def sigmoid(v):
    return 0.5 * jnp.tanh(0.5 * v) + 0.5


def channel_row(packed, k):
    return jnp.concatenate([packed[4 * k + b : 4 * k + b + 1, :] for b in range(4)], axis=1)


def pack(rows):
    pieces = [row[:, b * LANES : (b + 1) * LANES] for row in rows for b in range(4)]
    while len(pieces) % 8:
        pieces.append(jnp.zeros((1, LANES), f32))
    return jnp.concatenate(pieces, axis=0)


def spread(out_ref, packed):
    out_ref[...] = jnp.broadcast_to(packed[None], out_ref.shape)


def mask_of(count_ref):
    rows = lax.broadcasted_iota(jnp.int32, (CAP, COUT), 0)
    return (rows < count_ref[0, 0]).astype(f32)


def column_sum(v):
    return jnp.sum(v, axis=0, keepdims=True)


def moments(total_sum, total_square, positions):
    centre = total_sum / positions
    spread_value = total_square / positions - centre * centre
    return centre, lax.rsqrt(spread_value + epsilon)


def forward_taps(act_ref, w_ref, o):
    row_out, col_out = divmod(o, 2)
    total = None
    for row_in in range(2):
        tap = (row_in - row_out + 1) * 3 + (1 - col_out)
        part = dot(
            act_ref[:, pl.ds(row_in * 2 * COUT, 2 * COUT)], w_ref[pl.ds(tap * COUT, 2 * COUT), :]
        )
        total = part if total is None else total + part
    return total


def tap_of(i, o):
    return (i // 2 - o // 2 + 1) * 3 + (i % 2 - o % 2 + 1)


def backward_taps(dy_ref, w_ref, i):
    total = None
    for o in range(4):
        part = dot_nt(dy_ref[:, columns(o)], w_ref[pl.ds(tap_of(i, o) * COUT, COUT), :])
        total = part if total is None else total + part
    return total


def first_pairs(o):
    row_out, col_out = divmod(o, 2)
    runs = []
    for row_tap in range(3):
        row_in = 2 * row_out + row_tap - 1
        if 0 <= row_in < 4:
            col_tap = 1 if col_out == 0 else 0
            runs.append((row_in * 4 + 2 * col_out + col_tap - 1, row_tap * 3 + col_tap, 3 - col_tap))
    return runs


def k_first(x_ref, one_ref, count_ref, y1_ref, ys_ref, st_ref, local_ref, xb, wb, yb, sems):
    move = Mover(sems)
    lx = move.load(x_ref, xb)
    lw = move.load(one_ref.at[pl.ds(0, 10 * CIN)], wb)
    mask = mask_of(count_ref)
    lx.wait()
    lw.wait()
    sums = [0.0, 0.0, 0.0, 0.0]
    for o in range(4):
        total = None
        for cell, tap, cells in first_pairs(o):
            part = dot(xb[:, pl.ds(cell * CIN, cells * CIN)], wb[pl.ds(tap * CIN, cells * CIN), :])
            total = part if total is None else total + part
        yb[0, :, columns(o)] = total
        move.store(yb.at[0, :, columns(o)], y1_ref.at[:, columns(o)])
        valid = total * mask
        sums[0] += column_sum(valid)
        sums[1] += column_sum(valid * total)
        cell = (o // 2) * 8 + (o % 2) * 2
        total = dot(xb[:, pl.ds(cell * CIN, CIN)], wb[pl.ds(9 * CIN, CIN), :])
        yb[1, :, columns(o)] = total
        move.store(yb.at[1, :, columns(o)], ys_ref.at[:, columns(o)])
        valid = total * mask
        sums[2] += column_sum(valid)
        sums[3] += column_sum(valid * total)
    counted = jnp.full((8, LANES), count_ref[0, 0].astype(f32), f32)
    spread(st_ref, jnp.concatenate([pack(sums[:2]), counted], axis=0))
    local_ref[...] = pack(sums[2:])
    move.finish()


def k_second(
    y1_ref, recv_ref, norm_ref, local_ref, one_ref, count_ref, side_ref,
    mine_ref, theirs_ref, y2_ref, st_ref, keep_ref,
    yin, ab, at, tb, wb, yb, sems,
):
    move = Mover(sems)
    ly = [move.load(y1_ref.at[:, columns(o)], yin.at[:, columns(o)]) for o in range(4)]
    lw = move.load(one_ref.at[pl.ds(10 * CIN, 9 * COUT)], wb)
    got = jnp.sum(recv_ref[...], axis=0)
    total = got[8:9, 0:1]
    positions = 4.0 * total
    centre, inverse = moments(channel_row(got, 0), channel_row(got, 1), positions)
    keep_ref[...] = jnp.concatenate(
        [centre, inverse, jnp.broadcast_to(positions, (1, COUT)), jnp.zeros((5, COUT), f32)], axis=0
    )
    scale = norm_ref[0, 0:1, :] * inverse
    offset = norm_ref[1, 0:1, :] - centre * scale
    mask = mask_of(count_ref)
    for o in range(4):
        ly[o].wait()
        v = yin[:, columns(o)] * scale + offset
        ab[:, columns(o)] = (v * sigmoid(v)).astype(bf16)
        split_turn(at, tb, ab[:, columns(o)], o, COUT)
    hand_out(move, at, side_ref, mine_ref, theirs_ref)
    lw.wait()
    sums = [0.0, 0.0]
    for o in range(4):
        y = forward_taps(ab, wb, o)
        yb[:, columns(o)] = y
        move.store(yb.at[:, columns(o)], y2_ref.at[:, columns(o)])
        valid = y * mask
        sums[0] += column_sum(valid)
        sums[1] += column_sum(valid * y)
    spread(st_ref, jnp.concatenate([pack(sums), local_ref[...]], axis=0))
    move.finish()


def k_third(
    y2_ref, ys_ref, recv_ref, norm_ref, base_ref, two_ref, count_ref, side_ref,
    h1_ref, mine_ref, theirs_ref, y3_ref, st_ref, keep_ref,
    yin, sin, hout, ab, at, tb, wb, yb, sems,
):
    move = Mover(sems)
    ly, ls = [], []
    for o in range(4):
        ly.append(move.load(y2_ref.at[:, columns(o)], yin.at[:, columns(o)]))
        ls.append(move.load(ys_ref.at[:, columns(o)], sin.at[:, columns(o)]))
    lw = move.load(two_ref.at[pl.ds(0, 9 * COUT)], wb)
    got = jnp.sum(recv_ref[...], axis=0)
    positions = base_ref[2:3, :]
    c1, i1 = moments(channel_row(got, 0), channel_row(got, 1), positions)
    c2, i2 = moments(channel_row(got, 2), channel_row(got, 3), positions)
    keep_ref[...] = jnp.concatenate([c1, i1, c2, i2, jnp.zeros((4, COUT), f32)], axis=0)
    s1 = norm_ref[0, 1:2, :] * i1
    s2 = norm_ref[0, 2:3, :] * i2
    offset = norm_ref[1, 1:2, :] - c1 * s1 + (norm_ref[1, 2:3, :] - c2 * s2)
    mask = mask_of(count_ref)
    for o in range(4):
        ly[o].wait()
        ls[o].wait()
        v = yin[:, columns(o)] * s1 + sin[:, columns(o)] * s2 + offset
        h = v * sigmoid(v)
        hout[:, columns(o)] = h
        ab[:, columns(o)] = h.astype(bf16)
        move.store(hout.at[:, columns(o)], h1_ref.at[:, columns(o)])
        split_turn(at, tb, ab[:, columns(o)], o, COUT)
    hand_out(move, at, side_ref, mine_ref, theirs_ref)
    lw.wait()
    sums = [0.0, 0.0]
    for o in range(4):
        y = forward_taps(ab, wb, o)
        yb[:, columns(o)] = y
        move.store(yb.at[:, columns(o)], y3_ref.at[:, columns(o)])
        valid = y * mask
        sums[0] += column_sum(valid)
        sums[1] += column_sum(valid * y)
    spread(st_ref, pack(sums))
    move.finish()


def k_fourth(
    y3_ref, recv_ref, norm_ref, base_ref, two_ref, count_ref, side_ref,
    mine_ref, theirs_ref, y4_ref, st_ref, keep_ref,
    yin, ab, at, tb, wb, yb, sems,
):
    move = Mover(sems)
    ly = [move.load(y3_ref.at[:, columns(o)], yin.at[:, columns(o)]) for o in range(4)]
    lw = move.load(two_ref.at[pl.ds(9 * COUT, 9 * COUT)], wb)
    got = jnp.sum(recv_ref[...], axis=0)
    centre, inverse = moments(channel_row(got, 0), channel_row(got, 1), base_ref[2:3, :])
    keep_ref[...] = jnp.concatenate([centre, inverse, jnp.zeros((6, COUT), f32)], axis=0)
    scale = norm_ref[0, 3:4, :] * inverse
    offset = norm_ref[1, 3:4, :] - centre * scale
    mask = mask_of(count_ref)
    for o in range(4):
        ly[o].wait()
        v = yin[:, columns(o)] * scale + offset
        ab[:, columns(o)] = (v * sigmoid(v)).astype(bf16)
        split_turn(at, tb, ab[:, columns(o)], o, COUT)
    hand_out(move, at, side_ref, mine_ref, theirs_ref)
    lw.wait()
    sums = [0.0, 0.0]
    for o in range(4):
        y = forward_taps(ab, wb, o)
        yb[:, columns(o)] = y
        move.store(yb.at[:, columns(o)], y4_ref.at[:, columns(o)])
        valid = y * mask
        sums[0] += column_sum(valid)
        sums[1] += column_sum(valid * y)
    spread(st_ref, pack(sums))
    move.finish()


def k_heads(
    y4_ref, h1_ref, recv_ref, norm_ref, base_ref, head_ref, bias_ref, labels_ref, count_ref,
    pooled_ref, resid_ref, slope_ref, gram_ref, part_ref, keep_ref,
    yin, hin, sb, sems,
):
    move = Mover(sems)
    ly, lh = [], []
    for o in range(4):
        ly.append(move.load(y4_ref.at[:, columns(o)], yin.at[:, columns(o)]))
        lh.append(move.load(h1_ref.at[:, columns(o)], hin.at[:, columns(o)]))
    got = jnp.sum(recv_ref[...], axis=0)
    centre, inverse = moments(channel_row(got, 0), channel_row(got, 1), base_ref[2:3, :])
    keep_ref[...] = jnp.concatenate([centre, inverse, jnp.zeros((6, COUT), f32)], axis=0)
    scale = norm_ref[0, 4:5, :] * inverse
    offset = norm_ref[1, 4:5, :] - centre * scale
    total = None
    for o in range(4):
        ly[o].wait()
        lh[o].wait()
        v = yin[:, columns(o)] * scale + offset + hin[:, columns(o)]
        s = sigmoid(v)
        h = v * s
        sb[:, columns(o)] = s * (1.0 + v - h)
        move.store(sb.at[:, columns(o)], slope_ref.at[:, columns(o)])
        total = h if total is None else total + h
    pooled = total * 0.25
    pooled_ref[...] = pooled
    logits = dot(pooled, head_ref[...], highest) + bias_ref[...]
    labels = labels_ref[...]
    valid = (lax.broadcasted_iota(jnp.int32, (CAP, LANES), 0) < count_ref[0, 0]).astype(f32)
    resid = (sigmoid(logits) - labels) * valid
    resid_ref[...] = resid
    softplus = jnp.maximum(logits, 0.0) + jnp.log1p(jnp.exp(-jnp.abs(logits)))
    losses = valid * (softplus - labels * logits)
    gram = dot_tn(resid, resid, highest)
    lane = lax.broadcasted_iota(jnp.int32, (16, LANES), 1)
    packed = jnp.where(lane < TASKS, gram[0:16], jnp.where(lane < 2 * TASKS, gram[16:32], gram[32:48]))
    spread(gram_ref, packed)
    part_ref[...] = jnp.zeros(part_ref.shape, f32)
    for b in range(4):
        part_ref[pl.ds(b * TASKS, TASKS), :] = dot_tn(
            resid, pooled[:, b * LANES : (b + 1) * LANES], highest
        )[0:TASKS]
    ones = jnp.ones((CAP, LANES), f32)
    lane = lax.broadcasted_iota(jnp.int32, (TASKS, LANES), 1)
    part_ref[pl.ds(4 * TASKS, TASKS), :] = jnp.where(
        lane == 0, dot_tn(resid, ones, highest)[0:TASKS], dot_tn(losses, ones, highest)[0:TASKS]
    )
    move.finish()


def k_weights(
    recv_ref, square_ref, resid_ref, turned_ref, base_ref, keep_ref, part_ref, y4_ref, slope_ref, count_ref,
    weights_ref, u2_ref, st_ref,
    yin, sin, ub, sems,
):
    move = Mover(sems)
    ly, ls = [], []
    for o in range(4):
        ly.append(move.load(y4_ref.at[:, columns(o)], yin.at[:, columns(o)]))
        ls.append(move.load(slope_ref.at[:, columns(o)], sin.at[:, columns(o)]))
    total = base_ref[2:3, 0:1] * 0.25
    got = jnp.sum(recv_ref[...], axis=0)
    gram = jnp.concatenate(
        [
            got,
            pltpu.roll(got, LANES - TASKS, 1),
            pltpu.roll(got, LANES - 2 * TASKS, 1)[0:8],
        ],
        axis=0,
    )
    row_at = lax.broadcasted_iota(jnp.int32, (TASKS, LANES), 0)
    lane_at = lax.broadcasted_iota(jnp.int32, (TASKS, LANES), 1)
    gram = jnp.where(lane_at < TASKS, gram * square_ref[...], 0.0) / total
    trace = jnp.sum(
        jnp.sum(jnp.where(row_at == lane_at, gram, 0.0), axis=0, keepdims=True), axis=1, keepdims=True
    )
    scaled = gram / (trace / TASKS + 1e-06)
    live = lax.broadcasted_iota(jnp.int32, (1, LANES), 1) < TASKS
    weights = jnp.where(live, 1.0 / TASKS, 0.0)
    row = jnp.sum(scaled, axis=0, keepdims=True) / TASKS
    col = jnp.sum(scaled, axis=1, keepdims=True) / TASKS
    for turn in range(FW_STEPS):
        gamma = 2.0 / (turn + 3.0)
        low = jnp.min(col, axis=0, keepdims=True)
        grown_col = jnp.exp((low - col) / softness)
        grown_row = jnp.where(live, jnp.exp(jnp.where(live, (low - row) / softness, 0.0)), 0.0)
        share = gamma / jnp.sum(grown_col, axis=0, keepdims=True)
        weights = (1.0 - gamma) * weights + share * grown_row
        if turn + 1 < FW_STEPS:
            next_row = jnp.sum(scaled * grown_col, axis=0, keepdims=True)
            next_col = jnp.sum(scaled * grown_row, axis=1, keepdims=True)
            row = (1.0 - gamma) * row + share * next_row
            col = (1.0 - gamma) * col + share * next_col
    weights_ref[...] = jnp.broadcast_to(weights, (8, LANES))
    pooled_grad = dot(resid_ref[...] * (weights / total), turned_ref[...], highest) * 0.25
    centre, inverse = keep_ref[0:1, :], keep_ref[1:2, :]
    mask = mask_of(count_ref)
    sums = [0.0, 0.0]
    for o in range(4):
        ly[o].wait()
        ls[o].wait()
        u = pooled_grad * sin[:, columns(o)]
        ub[:, columns(o)] = u
        move.store(ub.at[:, columns(o)], u2_ref.at[:, columns(o)])
        valid = u * mask
        sums[0] += column_sum(valid * ((yin[:, columns(o)] - centre) * inverse))
        sums[1] += column_sum(valid)
    st_ref[:, 0:8, :] = jnp.broadcast_to(pack(sums)[None], part_ref.shape)
    st_ref[:, 8:16, :] = part_ref[...]
    move.finish()


def reverse_norm(g, y, mask, centre, inverse, gain, scale_total, shift_total, positions):
    xhat = (y - centre) * inverse
    return (gain * inverse) * (g - mask * ((shift_total + xhat * scale_total) / positions))


def k_back_fourth(
    u2_ref, y4_ref, recv_ref, norm_ref, base_ref, keep4_ref, two_ref, y3_ref, keep3_ref, count_ref,
    dy_ref, u3_ref, st_ref, tot_ref,
    uin, yin, zin, db, wb, ub, sems,
):
    move = Mover(sems)
    lu, ly = [], []
    for o in range(4):
        lu.append(move.load(u2_ref.at[:, columns(o)], uin.at[:, columns(o)]))
        ly.append(move.load(y4_ref.at[:, columns(o)], yin.at[:, columns(o)]))
    lw = move.load(two_ref.at[pl.ds(9 * COUT, 9 * COUT)], wb)
    lz = move.load(y3_ref, zin)
    got = jnp.sum(recv_ref[...], axis=0)
    tot_ref[...] = got[0:8]
    positions = base_ref[2:3, :]
    mask = mask_of(count_ref)
    scale_total, shift_total = channel_row(got, 0), channel_row(got, 1)
    for o in range(4):
        lu[o].wait()
        ly[o].wait()
        dy = reverse_norm(
            uin[:, columns(o)], yin[:, columns(o)], mask, keep4_ref[0:1, :], keep4_ref[1:2, :],
            norm_ref[0, 4:5, :], scale_total, shift_total, positions,
        )
        db[:, columns(o)] = dy.astype(bf16)
        move.store(db.at[:, columns(o)], dy_ref.at[:, columns(o)])
    lw.wait()
    lz.wait()
    centre, inverse = keep3_ref[0:1, :], keep3_ref[1:2, :]
    gain, shift = norm_ref[0, 3:4, :], norm_ref[1, 3:4, :]
    sums = [0.0, 0.0]
    for i in range(4):
        grad = backward_taps(db, wb, i)
        xhat = (zin[:, columns(i)] - centre) * inverse
        v = xhat * gain + shift
        s = sigmoid(v)
        u = grad * (s * (1.0 + v * (1.0 - s)))
        ub[:, columns(i)] = u
        move.store(ub.at[:, columns(i)], u3_ref.at[:, columns(i)])
        valid = u * mask
        sums[0] += column_sum(valid * xhat)
        sums[1] += column_sum(valid)
    spread(st_ref, jnp.concatenate([pack(sums), got[8:16]], axis=0))
    move.finish()


def k_back_third(
    u3_ref, y3_ref, recv_ref, norm_ref, base_ref, keep3_ref, two_ref, u2_ref, y2_ref, ys_ref, keep12_ref, count_ref,
    dy_ref, u1_ref, st_ref, tot_ref, head_ref,
    uin, yin, u2in, y2in, ysin, db, wb, ub, sems,
):
    move = Mover(sems)
    lu, ly = [], []
    for o in range(4):
        lu.append(move.load(u3_ref.at[:, columns(o)], uin.at[:, columns(o)]))
        ly.append(move.load(y3_ref.at[:, columns(o)], yin.at[:, columns(o)]))
    lw = move.load(two_ref.at[pl.ds(0, 9 * COUT)], wb)
    later = [move.load(u2_ref, u2in), move.load(y2_ref, y2in), move.load(ys_ref, ysin)]
    got = jnp.sum(recv_ref[:, 0:8, :], axis=0)
    tot_ref[...] = got
    head_ref[...] = recv_ref[:, 8:16, :]
    positions = base_ref[2:3, :]
    mask = mask_of(count_ref)
    scale_total, shift_total = channel_row(got, 0), channel_row(got, 1)
    for o in range(4):
        lu[o].wait()
        ly[o].wait()
        dy = reverse_norm(
            uin[:, columns(o)], yin[:, columns(o)], mask, keep3_ref[0:1, :], keep3_ref[1:2, :],
            norm_ref[0, 3:4, :], scale_total, shift_total, positions,
        )
        db[:, columns(o)] = dy.astype(bf16)
        move.store(db.at[:, columns(o)], dy_ref.at[:, columns(o)])
    lw.wait()
    for copy in later:
        copy.wait()
    c1, i1, c2, i2 = (keep12_ref[k : k + 1, :] for k in range(4))
    g1, g2 = norm_ref[0, 1:2, :], norm_ref[0, 2:3, :]
    shift = norm_ref[1, 1:2, :] + norm_ref[1, 2:3, :]
    sums = [0.0, 0.0, 0.0]
    for i in range(4):
        grad = backward_taps(db, wb, i) + u2in[:, columns(i)]
        x1 = (y2in[:, columns(i)] - c1) * i1
        x2 = (ysin[:, columns(i)] - c2) * i2
        v = x1 * g1 + x2 * g2 + shift
        s = sigmoid(v)
        u = grad * (s * (1.0 + v * (1.0 - s)))
        ub[:, columns(i)] = u
        move.store(ub.at[:, columns(i)], u1_ref.at[:, columns(i)])
        valid = u * mask
        sums[0] += column_sum(valid * x1)
        sums[1] += column_sum(valid * x2)
        sums[2] += column_sum(valid)
    spread(st_ref, pack(sums))
    move.finish()


def k_back_second(
    u1_ref, y2_ref, ys_ref, recv_ref, norm_ref, base_ref, keep12_ref, one_ref, y1_ref, count_ref,
    dy2_ref, dys_ref, u0_ref, st_ref, tot_ref,
    uin, y2in, ysin, y1in, db, dsb, wb, ub, sems,
):
    move = Mover(sems)
    first = []
    for o in range(4):
        first.append(
            [
                move.load(ref.at[:, columns(o)], buf.at[:, columns(o)])
                for ref, buf in ((u1_ref, uin), (y2_ref, y2in), (ys_ref, ysin))
            ]
        )
    lw = move.load(one_ref.at[pl.ds(10 * CIN, 9 * COUT)], wb)
    ly1 = move.load(y1_ref, y1in)
    got = jnp.sum(recv_ref[...], axis=0)
    tot_ref[...] = got
    positions = base_ref[2:3, :]
    mask = mask_of(count_ref)
    scale1, scale2, shift_total = (channel_row(got, k) for k in range(3))
    c1, i1, c2, i2 = (keep12_ref[k : k + 1, :] for k in range(4))
    for o in range(4):
        for copy in first[o]:
            copy.wait()
        u = uin[:, columns(o)]
        dy2 = reverse_norm(
            u, y2in[:, columns(o)], mask, c1, i1, norm_ref[0, 1:2, :], scale1, shift_total, positions
        )
        db[:, columns(o)] = dy2.astype(bf16)
        move.store(db.at[:, columns(o)], dy2_ref.at[:, columns(o)])
        dys = reverse_norm(
            u, ysin[:, columns(o)], mask, c2, i2, norm_ref[0, 2:3, :], scale2, shift_total, positions
        )
        dsb[:, columns(o)] = dys.astype(bf16)
        move.store(dsb.at[:, columns(o)], dys_ref.at[:, columns(o)])
    lw.wait()
    ly1.wait()
    centre, inverse = base_ref[0:1, :], base_ref[1:2, :]
    gain, shift = norm_ref[0, 0:1, :], norm_ref[1, 0:1, :]
    sums = [0.0, 0.0]
    for i in range(4):
        grad = backward_taps(db, wb, i)
        xhat = (y1in[:, columns(i)] - centre) * inverse
        v = xhat * gain + shift
        s = sigmoid(v)
        u = grad * (s * (1.0 + v * (1.0 - s)))
        ub[:, columns(i)] = u
        move.store(ub.at[:, columns(i)], u0_ref.at[:, columns(i)])
        valid = u * mask
        sums[0] += column_sum(valid * xhat)
        sums[1] += column_sum(valid)
    spread(st_ref, pack(sums))
    move.finish()


def k_back_first(
    u0_ref, y1_ref, recv_ref, norm_ref, base_ref, count_ref, dy_ref, tot_ref, uin, yin, db, sems
):
    move = Mover(sems)
    lu, ly = [], []
    for o in range(4):
        lu.append(move.load(u0_ref.at[:, columns(o)], uin.at[:, columns(o)]))
        ly.append(move.load(y1_ref.at[:, columns(o)], yin.at[:, columns(o)]))
    got = jnp.sum(recv_ref[...], axis=0)
    tot_ref[...] = got
    positions = base_ref[2:3, :]
    mask = mask_of(count_ref)
    scale_total, shift_total = channel_row(got, 0), channel_row(got, 1)
    for o in range(4):
        lu[o].wait()
        ly[o].wait()
        dy = reverse_norm(
            uin[:, columns(o)], yin[:, columns(o)], mask, base_ref[0:1, :], base_ref[1:2, :],
            norm_ref[0, 0:1, :], scale_total, shift_total, positions,
        )
        db[:, columns(o)] = dy.astype(bf16)
        move.store(db.at[:, columns(o)], dy_ref.at[:, columns(o)])
    move.finish()


def k_turn(x_ref, side_ref, mine_ref, theirs_ref, xb, at, tb, sems):
    move = Mover(sems)
    loads = [
        move.load(x_ref.at[:, columns(o)], xb.at[:, columns(o)]) for o in range(16 * CIN // COUT)
    ]
    for cell in range(16):
        if cell % 2 == 0:
            loads[cell // 2].wait()
        split_turn(at, tb, xb[:, pl.ds(cell * CIN, CIN)], cell, CIN)
    hand_out(move, at, side_ref, mine_ref, theirs_ref)
    move.finish()


def pair_taps(move, lefts, rights, gb, grads_ref, base, half, side_in, stride):
    for tap in range(9):
        total = None
        for o in range(4):
            row_in = stride * (o // 2) + tap // 3 - 1
            col_in = stride * (o % 2) + tap % 3 - 1
            if not (0 <= row_in < side_in and 0 <= col_in < side_in):
                continue
            cell = row_in * side_in + col_in
            for left, right in zip(lefts, rights):
                part = dot(left[pl.ds(cell * half, half), :], right[:, columns(o)])
                total = part if total is None else total + part
        gb[pl.ds(tap * half, half), :] = total.astype(bf16)
        move.store(gb.at[pl.ds(tap * half, half)], grads_ref.at[pl.ds(base + tap * half, half)])


def k_pair_grad(
    mine_ref, got_ref, dy_ref, dyg_ref, grads_ref, mb, ob, db, dgb, gb, sems
):
    move = Mover(sems)
    loads = [
        move.load(src, dst)
        for src, dst in ((mine_ref, mb), (dy_ref, db), (got_ref, ob), (dyg_ref, dgb))
    ]
    for copy in loads:
        copy.wait()
    pair_taps(move, (mb, ob), (db, dgb), gb, grads_ref, 0, COUT // 2, 2, 1)
    move.finish()


def k_pair_second(
    mine_ref, got_ref, dy_ref, dyg_ref, xm_ref, xg_ref, dys_ref, dysg_ref, grads_ref,
    mb, ob, db, dgb, gb, xmb, xgb, dsb, dsgb, gsb, sems,
):
    move = Mover(sems)
    half = CIN // 2
    loads = [
        move.load(src, dst)
        for src, dst in ((mine_ref, mb), (dy_ref, db), (got_ref, ob), (dyg_ref, dgb))
    ]
    later = [move.load(dys_ref, dsb), move.load(dysg_ref, dsgb)]
    for o in range(4):
        cell = (o // 2) * 8 + (o % 2) * 2
        for src, dst in ((xm_ref, xmb), (xg_ref, xgb)):
            later.append(move.load(src.at[pl.ds(cell * half, half)], dst.at[pl.ds(o * half, half)]))
    for copy in loads:
        copy.wait()
    pair_taps(move, (mb, ob), (db, dgb), gb, grads_ref, 10 * half, COUT // 2, 2, 1)
    for copy in later:
        copy.wait()
    total = None
    for o in range(4):
        for left, right in ((xmb, dsb), (xgb, dsgb)):
            part = dot(left[pl.ds(o * half, half), :], right[:, columns(o)])
            total = part if total is None else total + part
    gsb[...] = total.astype(bf16)
    move.store(gsb, grads_ref.at[pl.ds(9 * half, half)])
    move.finish()


def k_pair_first(
    xm_ref, xg_ref, dy_ref, dyg_ref, gone_ref, grads_ref, mb, ob, db, dgb, gb, sems
):
    del gone_ref
    move = Mover(sems)
    loads = [
        move.load(src, dst)
        for src, dst in ((xm_ref, mb), (dy_ref, db), (xg_ref, ob), (dyg_ref, dgb))
    ]
    for copy in loads:
        copy.wait()
    pair_taps(move, (mb, ob), (db, dgb), gb, grads_ref, 0, CIN // 2, 4, 2)
    move.finish()


def k_input_grad(dy_ref, dys_ref, one_ref, dx_ref, db, dsb, wb, xb, sems):
    move = Mover(sems)
    loads = [
        move.load(one_ref.at[pl.ds(0, 10 * CIN)], wb),
        move.load(dy_ref, db),
        move.load(dys_ref, dsb),
    ]
    for copy in loads:
        copy.wait()
    for cell in range(16):
        row_in, col_in = divmod(cell, 4)
        total = None
        for o in range(4):
            row_tap, col_tap = row_in - 2 * (o // 2) + 1, col_in - 2 * (o % 2) + 1
            if not (0 <= row_tap < 3 and 0 <= col_tap < 3):
                continue
            part = dot_nt(db[:, columns(o)], wb[pl.ds((row_tap * 3 + col_tap) * CIN, CIN), :])
            total = part if total is None else total + part
        if row_in % 2 == 0 and col_in % 2 == 0:
            o = (row_in // 2) * 2 + col_in // 2
            total = total + dot_nt(dsb[:, columns(o)], wb[pl.ds(9 * CIN, CIN), :])
        xb[:, pl.ds(cell * CIN, CIN)] = total
        move.store(xb.at[:, pl.ds(cell * CIN, CIN)], dx_ref.at[:, pl.ds(cell * CIN, CIN)])
    move.finish()


def nesterov(grad, master, momentum, average, rate):
    moment = momentum_decay * momentum + grad
    fresh = master - rate * (grad + momentum_decay * moment)
    return (moment, fresh, average_decay * average + (1.0 - average_decay) * fresh)


def exchange(packed):
    return lax.all_to_all(packed, AXES, 0, 0, tiled=True)


def swap(value, devices, bits):
    return lax.ppermute(value, AXES, [(i, i ^ bits) for i in range(devices)])


def part_of(value, index, axis):
    return lax.dynamic_index_in_dim(value, index, axis, keepdims=False)


def add(left, right):
    return (left.astype(f32) + right.astype(f32)).astype(bf16)


class Grid:
    def __init__(self, devices):
        self.devices = devices
        number = lax.axis_index("batch") * lax.axis_size("pass") + lax.axis_index("pass")
        self.side, self.x, self.y, self.z = (
            number % 2,
            (number // 2) % 2,
            (number // 4) % 2,
            number // 8,
        )

    def swap(self, value, bits):
        return swap(value, self.devices, bits)


def scatter_plane(grid, grads):
    half = COUT // 2
    left, right = grads[..., :half], grads[..., half:]
    got_left = grid.swap(part_of(left, 1 - grid.x, 2), 2)
    got_right = grid.swap(part_of(right, 1 - grid.y, 1), 4)
    left = add(part_of(left, grid.x, 2), got_left)
    right = add(part_of(right, grid.y, 1), got_right)
    got_left = grid.swap(part_of(left, 1 - grid.y, 1), 4)
    got_right = grid.swap(part_of(right, 1 - grid.x, 1), 2)
    return jnp.concatenate(
        [
            add(part_of(left, grid.y, 1), got_left),
            add(part_of(right, grid.x, 1), got_right),
        ],
        axis=-1,
    )


def scatter_line(grid, value):
    total = part_of(value, grid.z, 0).astype(f32)
    for other in (1, 2, 3):
        total = total + grid.swap(part_of(value, grid.z ^ other, 0), other * 8).astype(f32)
    got = grid.swap(part_of(total, 1 - grid.side, 0).astype(bf16), 1).astype(f32)
    own = part_of(total, grid.side, 0)
    rows = own.shape[0]
    own, got = (v.reshape(rows // 16, 16, COUT) for v in (own, got))
    first = jnp.where(grid.side == 0, own, got)
    second = jnp.where(grid.side == 0, got, own)
    return jnp.stack([first, second], axis=1).reshape(2 * rows, COUT)


def reduce_halves(devices, side, half_grad):
    groups = half_grad.reshape(-1, 16, COUT)
    empty = jnp.zeros_like(groups)
    full = jnp.stack(
        [jnp.where(side == 0, groups, empty), jnp.where(side == 0, empty, groups)], axis=1
    ).reshape(-1, COUT)
    return lax.psum_scatter(full, AXES, scatter_dimension=0, tiled=True).astype(f32)


def make_shards(devices, fast):
    def shards(
        features,
        labels,
        image_counts,
        block_one_master,
        block_one_momentum,
        block_one_average,
        block_two_master,
        block_two_momentum,
        block_two_average,
        norm_params,
        norm_momentum,
        norm_average,
        head_params,
        head_momentum,
        head_average,
    ):
        images_all = CAP * devices
        count = image_counts
        side = (lax.axis_index("pass") % 2).astype(jnp.int32).reshape(1, 1)
        one = lax.all_gather(block_one_master.astype(bf16), AXES, axis=0, tiled=True)
        two = lax.all_gather(block_two_master.astype(bf16), AXES, axis=0, tiled=True)
        x = features.reshape(CAP, 16 * CIN)

        rows_one, rows_two = one.shape[0], two.shape[0]
        wide_f, wide_b = shape((CAP, WIDE), f32), shape((CAP, WIDE), bf16)
        wf, wb16 = pltpu.VMEM((CAP, WIDE), f32), pltpu.VMEM((CAP, WIDE), bf16)
        weight = pltpu.VMEM((9 * COUT, COUT), bf16)
        small = shape((8, COUT), f32)
        packed8, packed16 = shape((8, LANES), f32), shape((16, LANES), f32)
        send8, send16 = shape((devices, 8, LANES), f32), shape((devices, 16, LANES), f32)

        def sems(n):
            return pltpu.SemaphoreType.DMA((n,))

        conv_flops = 2 * 16 * CAP * COUT * COUT
        first_flops = 2 * 29 * CAP * CIN * COUT
        head_rows = head_params[:COUT]
        pad = LANES - 3 * TASKS

        def thrice(v):
            return jnp.concatenate([v, v, v, jnp.zeros((v.shape[0], pad), v.dtype)], axis=1)

        head_wide = thrice(head_rows)
        bias_wide = thrice(head_params[COUT:])
        labels_wide = thrice(labels.astype(f32))
        turned = jnp.pad(head_rows.T, ((0, LANES - TASKS), (0, 0)))
        square = jnp.pad(
            jnp.dot(head_rows.T, head_rows, precision=highest), ((0, 0), (0, LANES - TASKS))
        )

        turned_half = shape((WIDE // 2, CAP), bf16)
        turn_scratch = [pltpu.VMEM((2, WIDE // 2, CAP), bf16), pltpu.VMEM((COUT, CAP), bf16)]

        def sibling(value):
            return swap(value, devices, 1)

        x_mine, x_theirs = run(
            k_turn,
            (x, side),
            [HBM, SMEM],
            [shape((8 * CIN, CAP), bf16)] * 2,
            [HBM, HBM],
            [
                pltpu.VMEM((CAP, 16 * CIN), bf16),
                pltpu.VMEM((2, 8 * CIN, CAP), bf16),
                pltpu.VMEM((COUT, CAP), bf16),
                sems(10),
            ],
            0,
            4_000_000,
            name="turn_features",
        )
        x_got = sibling(x_theirs)
        y1, ys, st, local = run(
            k_first,
            (x, one, count),
            [HBM, HBM, SMEM],
            [wide_f, wide_f, send16, packed8],
            [HBM, HBM, VMEM, VMEM],
            [
                pltpu.VMEM((CAP, 16 * CIN), bf16),
                pltpu.VMEM((10 * CIN, COUT), bf16),
                pltpu.VMEM((2, CAP, WIDE), f32),
                sems(10),
            ],
            first_flops,
            9_000_000,
            name="first_conv",
        )
        got = exchange(st)
        a1_mine, a1_theirs, y2, st, keep0 = run(
            k_second,
            (y1, got, norm_params, local, one, count, side),
            [HBM, VMEM, VMEM, VMEM, HBM, SMEM, SMEM],
            [turned_half, turned_half, wide_f, send16, small],
            [HBM, HBM, HBM, VMEM, VMEM],
            [wf, wb16, *turn_scratch, weight, wf, sems(11)],
            conv_flops,
            10_000_000,
            name="second_conv",
        )
        got = exchange(st)
        a1_got = sibling(a1_theirs)
        h1, hb_mine, hb_theirs, y3, st, keep12 = run(
            k_third,
            (y2, ys, got, norm_params, keep0, two, count, side),
            [HBM, HBM, VMEM, VMEM, VMEM, HBM, SMEM, SMEM],
            [wide_f, turned_half, turned_half, wide_f, send8, small],
            [HBM, HBM, HBM, HBM, VMEM, VMEM],
            [wf, wf, wf, wb16, *turn_scratch, weight, wf, sems(19)],
            conv_flops,
            14_000_000,
            name="third_conv",
        )
        got = exchange(st)
        hb_got = sibling(hb_theirs)
        a3_mine, a3_theirs, y4, st, keep3 = run(
            k_fourth,
            (y3, got, norm_params, keep0, two, count, side),
            [HBM, VMEM, VMEM, VMEM, HBM, SMEM, SMEM],
            [turned_half, turned_half, wide_f, send8, small],
            [HBM, HBM, HBM, VMEM, VMEM],
            [wf, wb16, *turn_scratch, weight, wf, sems(11)],
            conv_flops,
            10_000_000,
            name="fourth_conv",
        )
        got = exchange(st)
        a3_got = sibling(a3_theirs)
        wide_lanes = shape((CAP, LANES), f32)
        pooled, resid, slope, st, part, keep4 = run(
            k_heads,
            (y4, h1, got, norm_params, keep0, head_wide, bias_wide, labels_wide, count),
            [HBM, HBM, VMEM, VMEM, VMEM, VMEM, VMEM, VMEM, SMEM],
            [
                shape((CAP, COUT), f32),
                wide_lanes,
                wide_f,
                send16,
                shape((8 * devices, LANES), f32),
                small,
            ],
            [VMEM, VMEM, HBM, VMEM, VMEM, VMEM],
            [wf, wf, wf, sems(12)],
            1_000_000_000,
            7_000_000,
            name="heads",
        )
        got = exchange(st)
        weights, u2, st = run(
            k_weights,
            (
                got, square, resid, turned, keep0, keep4, part.reshape(devices, 8, LANES), y4, slope, count,
            ),
            [VMEM, VMEM, VMEM, VMEM, VMEM, VMEM, VMEM, HBM, HBM, SMEM],
            [packed8, wide_f, send16],
            [VMEM, HBM, VMEM],
            [wf, wf, wf, sems(12)],
            1_000_000_000,
            7_000_000,
            name="task_weights",
        )

        got = exchange(st)
        dy4, u3, st, tot4 = run(
            k_back_fourth,
            (u2, y4, got, norm_params, keep0, keep4, two, y3, keep3, count),
            [HBM, HBM, VMEM, VMEM, VMEM, VMEM, HBM, HBM, VMEM, SMEM],
            [wide_b, wide_f, send16, packed8],
            [HBM, HBM, VMEM, VMEM],
            [wf, wf, wf, wb16, weight, wf, sems(18)],
            conv_flops,
            14_000_000,
            name="fourth_back",
        )
        got = exchange(st)
        half_rows = 9 * COUT // 2
        half_turned = pltpu.VMEM((WIDE // 2, CAP), bf16)
        pair_scratch = [half_turned, half_turned, wb16, wb16, pltpu.VMEM((half_rows, COUT), bf16)]

        def pair_grad(mine, theirs, dy, dy_got, name):
            return run(
                k_pair_grad,
                (mine, theirs, dy, dy_got),
                [HBM] * 4,
                shape((half_rows, COUT), bf16),
                HBM,
                [*pair_scratch, sems(13)],
                conv_flops,
                6_000_000,
                name=name,
            )

        grads_four = pair_grad(a3_mine, a3_got, dy4, sibling(dy4), "fourth_weights")
        dy3, u1, st, tot3, head_sum = run(
            k_back_third,
            (u3, y3, got, norm_params, keep0, keep3, two, u2, y2, ys, keep12, count),
            [HBM, HBM, VMEM, VMEM, VMEM, VMEM, HBM, HBM, HBM, HBM, VMEM, SMEM],
            [wide_b, wide_f, send16, packed8, send8],
            [HBM, HBM, VMEM, VMEM, VMEM],
            [wf, wf, wf, wf, wf, wb16, weight, wf, sems(20)],
            conv_flops,
            18_000_000,
            name="third_back",
        )
        got = exchange(st)
        grads_three = pair_grad(hb_mine, hb_got, dy3, sibling(dy3), "third_weights")
        dy2, dys, u0, st, tot12 = run(
            k_back_second,
            (u1, y2, ys, got, norm_params, keep0, keep12, one, y1, count),
            [HBM, HBM, HBM, VMEM, VMEM, VMEM, VMEM, HBM, HBM, SMEM],
            [wide_b, wide_b, wide_f, send8, packed16],
            [HBM, HBM, HBM, VMEM, VMEM],
            [wf, wf, wf, wf, wb16, wb16, weight, wf, sems(26)],
            conv_flops,
            18_000_000,
            name="second_back",
        )
        got = exchange(st)
        dys_got = sibling(dys)
        grads_one = run(
            k_pair_second,
            (a1_mine, a1_got, dy2, sibling(dy2), x_mine, x_got, dys, dys_got),
            [HBM] * 8,
            shape((rows_one // 2, COUT), bf16),
            HBM,
            [
                *pair_scratch,
                pltpu.VMEM((2 * CIN, CAP), bf16),
                pltpu.VMEM((2 * CIN, CAP), bf16),
                wb16,
                wb16,
                pltpu.VMEM((CIN // 2, COUT), bf16),
                sems(24),
            ],
            conv_flops,
            9_000_000,
            name="second_weights",
        )
        dy1, tot0 = run(
            k_back_first,
            (u0, y1, got, norm_params, keep0, count),
            [HBM, HBM, VMEM, VMEM, VMEM, SMEM],
            [wide_b, packed8],
            [HBM, VMEM],
            [wf, wf, wb16, sems(12)],
            0,
            5_000_000,
            name="first_back",
        )
        half_features = pltpu.VMEM((8 * CIN, CAP), bf16)
        grads_one = run(
            k_pair_first,
            (x_mine, x_got, dy1, sibling(dy1), grads_one),
            [HBM] * 5,
            shape((rows_one // 2, COUT), bf16),
            HBM,
            [
                half_features,
                half_features,
                wb16,
                wb16,
                pltpu.VMEM((9 * CIN // 2, COUT), bf16),
                sems(13),
            ],
            first_flops,
            8_000_000,
            {4: 0},
            name="first_weights",
        )
        if fast:
            grid = Grid(devices)
            rows = rows_two // devices // 2
            planes = [
                scatter_plane(grid, g.reshape(2, 2, 2, 2, rows, COUT))
                for g in (grads_three, grads_four)
            ]
            two_sum = scatter_line(grid, jnp.concatenate(planes, axis=0))
            rows = rows_one // devices // 2
            one_sum = scatter_line(
                grid, scatter_plane(grid, grads_one.reshape(4, 2, 2, 2, rows, COUT))
            )
        else:
            two_sum = reduce_halves(
                devices, side[0, 0], jnp.concatenate([grads_three, grads_four], axis=0)
            )
            one_sum = reduce_halves(devices, side[0, 0], grads_one)
        dx = run(
            k_input_grad,
            (dy1, dys, one),
            [HBM, HBM, HBM],
            shape((CAP, 16 * CIN), f32),
            HBM,
            [
                wb16,
                wb16,
                pltpu.VMEM((10 * CIN, COUT), bf16),
                pltpu.VMEM((CAP, 16 * CIN), f32),
                sems(19),
            ],
            first_flops,
            9_000_000,
            name="input_grad",
        )
        input_grad = dx.reshape(CAP, 4, 4, CIN)

        def unpacked(packed):
            return packed.reshape(-1, COUT)

        t0, t3, t4, t12 = unpacked(tot0), unpacked(tot3), unpacked(tot4), unpacked(tot12)
        norm_grad = jnp.stack(
            [
                jnp.stack([t0[0], t12[0], t12[1], t3[0], t4[0]]),
                jnp.stack([t0[1], t12[2], t12[2], t3[1], t4[1]]),
            ]
        )
        total = keep0[2, 0] * 0.25
        head_sum = head_sum.reshape(-1, LANES)[: 5 * TASKS].reshape(5, TASKS, LANES)
        task_losses = head_sum[4, :, 1] / total
        head_grad = jnp.concatenate(
            [head_sum[:4].transpose(0, 2, 1).reshape(COUT, TASKS), head_sum[4, :, 0][None]], axis=0
        ) / total
        scale_rate = math.sqrt(images_all)
        one_m, one_w, one_a = nesterov(
            one_sum,
            block_one_master,
            block_one_momentum,
            block_one_average,
            rate_conv * scale_rate,
        )
        two_m, two_w, two_a = nesterov(
            two_sum,
            block_two_master,
            block_two_momentum,
            block_two_average,
            rate_conv * scale_rate,
        )
        norm_m, norm_w, norm_a = nesterov(
            norm_grad, norm_params, norm_momentum, norm_average, rate_norm * scale_rate
        )
        head_m, head_w, head_a = nesterov(
            head_grad, head_params, head_momentum, head_average, rate_head * scale_rate
        )
        return (
            pooled,
            input_grad,
            task_losses,
            weights[0, :TASKS],
            one_m,
            one_w,
            one_a,
            one_w.astype(bf16),
            two_m,
            two_w,
            two_a,
            two_w.astype(bf16),
            norm_m,
            norm_w,
            norm_a,
            head_m,
            head_w,
            head_a,
        )

    return shards


def solution(mesh):
    devices = mesh.shape["batch"] * mesh.shape["pass"]
    fast = mesh.shape["batch"] == 8 and mesh.shape["pass"] == 4
    rows = P(AXES, None)
    in_specs = (
        P(AXES, None, None, None),
        rows,
        P("batch", "pass"),
        rows,
        rows,
        rows,
        rows,
        rows,
        rows,
        P(),
        P(),
        P(),
        P(),
        P(),
        P(),
    )
    out_specs = (
        rows,
        P(AXES, None, None, None),
        P(),
        P(),
        rows,
        rows,
        rows,
        rows,
        rows,
        rows,
        rows,
        rows,
        P(),
        P(),
        P(),
        P(),
        P(),
        P(),
    )
    return jax.shard_map(
        make_shards(devices, fast), mesh=mesh, in_specs=in_specs, out_specs=out_specs, check_vma=False
    )
```

time: 1410 us -> 501 us (0.36)
  matrix products: 356 us -> 0.21 us
  blocking collectives: 361 us -> 32.9 us
  local copies, waits for them, and re-layouts: 313 us -> 38 us
  other arithmetic: 159 us -> 19.1 us
  Pallas kernels: 0 us -> 114 us
  starting transfers between devices: 0.21 us -> 47.5 us
  waiting for transfers between devices: 190 us -> 224 us
    psum x9 -> x0, blocking collectives: 361 us -> none  [the longest x4 161 us: norm_reverse(): lax.psum((partial_scale, shift_part), ('batch', 'pass'))]
    dot_general x49 -> x1, matrix products: 356 us -> 0.21 us  [shards(): jnp.dot(head_rows.T, head_rows, precision=highest)]
    reduce_scatter x2 -> x0, waiting for transfers between devices: 117 us -> none  [reduce_rows(): lax.psum_scatter(full_grad, ('batch', 'pass'), scatter_dimension=0, tiled...]
    pallas_call x0 -> x16, Pallas kernels: none -> 114 us  [run(): pl.pallas_call(body, out_shape=outs, in_specs=in_specs, out_specs=out_spe...]
    unnamed x225 -> x75, local copies, waits for them, and re-layouts: 120 us -> 13.5 us
    reshape x13 -> x3, local copies, waits for them, and re-layouts: 78 us -> 8.79 us  [the longest x1 6.02 us: shards(): input_grad = dx.reshape(CAP, 4, 4, CIN)]
    dot_general x12 -> x0, local copies, waits for them, and re-layouts: 66.2 us -> none  [the longest x5 48 us: collect_weight_grad(): jnp.einsum('iot,icod->tcd', jnp.asarray(table, jnp.float32), dense, preci...]
    ppermute x0 -> x29, waiting for transfers between devices: none -> 65.1 us  [swap(): return lax.ppermute(value, AXES, [(i, i ^ bits) for i in range(devices)])]
  transfers between devices with their start and end apart: 5 -> 38, of which waited for: 2 -> 22; matrix products, arithmetic and copies ran while one was open for 45% -> 10% of each run, Pallas kernels for 0% -> 15%
where the time goes in v1:
time: 501 us; the launch traced here: 491 us
  waiting for transfers between devices  224 us (45%)
  Pallas kernels  114 us (23%)
  starting transfers between devices  47.5 us (9%)
  local copies, waits for them, and re-layouts  38 us (8%)
  blocking collectives  32.9 us (7%)
  other arithmetic  19.1 us (4%)
  between operations  16.4 us (3%)
    pallas_call x16, Pallas kernels, run(): pl.pallas_call(body, out_shape=outs, in_specs=in_specs, out_specs=out_spe...  114 us
    all_gather x1, waiting for transfers between devices, shards(): lax.all_gather(block_one_master.astype(bf16), AXES, axis=0, tiled=True)  73.2 us
    ppermute x29, waiting for transfers between devices, swap(): return lax.ppermute(value, AXES, [(i, i ^ bits) for i in range(devices)])  65.1 us
    all_to_all x7, waiting for transfers between devices, exchange(): return lax.all_to_all(packed, AXES, 0, 0, tiled=True)  46 us
    all_gather x1, waiting for transfers between devices, shards(): lax.all_gather(block_two_master.astype(bf16), AXES, axis=0, tiled=True)  39.3 us
    all_to_all x2, blocking collectives, exchange(): return lax.all_to_all(packed, AXES, 0, 0, tiled=True)  32.9 us
    ppermute x29, starting transfers between devices, swap(): return lax.ppermute(value, AXES, [(i, i ^ bits) for i in range(devices)])  26.5 us
    all_to_all x7, starting transfers between devices, exchange(): return lax.all_to_all(packed, AXES, 0, 0, tiled=True)  21 us
  transfers between devices with their start and end apart: 38, of which 22 were waited for; matrix products, arithmetic and copies ran while one was open for 10% of the time, Pallas kernels for 15%

profile of v1, /device:TPU:0, one launch (start us, length us, event | category | flops | bytes accessed | tf_op | source)
XLA Modules:
  0.0 491.3 jit_solution(14837141223759241875)
XLA Ops:
  14.5 73.2 %all-gather.3.cloned.1.call-done.one_ref = bf16[7168,512]{1,0:T(8,128)(2,1)} async-done(((bf16[224,512]{1,0:T(8,128)(2,1)}), bf16[7168,512]{1,0:T(8,128)(2,1)}) %all-gather.3.cloned.1.call-update) | async-done | bytes 7340048 | tf_op jit(solution)/shard_map/all_gather | solution.py:828
  87.7 6.3 %first_conv.1 = (f32[256,2048]{1,0:T(8,128)}, f32[256,2048]{1,0:T(8,128)}, f32[32,16,128]{2,1,0:T(8,128)}, f32[8,128]{1,0:T(8,128)}) custom-call(bf16[256,4096]{1,0:T(8,128)(2,1)} %reshape.208.x_ref, bf16[7168,512]{1,0:T(8,128)(2,1)} %all-gather.3.cloned.1.call-done.one_ref, s32[1,1]{1,0:T(1,128)S(6)} %copy.168.count_ref), custom_call_target="tpu_custom_call" | custom-call | flops 1946157056 | bytes 9000000 | tf_op jit(solution)/shard_map/first_conv/pallas_call | solution.py:40
  97.8 13.2 %all-to-all-done.recv_ref = f32[32,16,128]{2,1,0:T(8,128)S(1)} async-done(((f32[32,16,128]{2,1,0:T(8,128)}), f32[32,16,128]{2,1,0:T(8,128)S(1)}, u32[]{:S(2)}, u32[]{:S(2)}) %all-to-all-start) | async-done | bytes 262176 | tf_op jit(solution)/shard_map/all_to_all | solution.py:737
  111.6 8.4 %second_conv.1 = (bf16[1024,256]{1,0:T(8,128)(2,1)}, bf16[1024,256]{1,0:T(8,128)(2,1)}, f32[256,2048]{1,0:T(8,128)}, f32[32,16,128]{2,1,0:T(8,128)}, f32[8,512]{1,0:T(8,128)}) custom-call(f32[256,2048]{1,0:T(8,128)} %get-tuple-element.65.y1_ref, f32[32,16,128]{2,1,0:T(8,128)} %copy-done.12, f32[2,5,512]{2,1,0:T(8,128)} %copy.86.norm_ref, ...), custom_call_target="tpu_custom_call" | custom-call | flops 2147483648 | bytes 10000000 | tf_op jit(solution)/shard_map/second_conv/pallas_call | solution.py:40
  120.0 19.0 %all_to_all.45.recv_ref = f32[32,16,128]{2,1,0:T(8,128)} all-to-all(f32[32,16,128]{2,1,0:T(8,128)} %get-tuple-element.70), channel_id=1, replica_groups=mesh['batch'=8,'pass'=4] {'batch','pass'}, dimensions={0} | all-to-all | bytes 524288 | tf_op jit(solution)/shard_map/all_to_all | solution.py:737
  139.0 39.3 %all-gather.5.cloned.1.call-done.two_ref = bf16[9216,512]{1,0:T(8,128)(2,1)} async-done(((bf16[288,512]{1,0:T(8,128)(2,1)}), bf16[9216,512]{1,0:T(8,128)(2,1)}) %all-gather.5.cloned.1.call-update) | async-done | bytes 9437200 | tf_op jit(solution)/shard_map/all_gather | solution.py:829
  178.4 9.8 %third_conv.1 = (f32[256,2048]{1,0:T(8,128)}, bf16[1024,256]{1,0:T(8,128)(2,1)}, bf16[1024,256]{1,0:T(8,128)(2,1)}, f32[256,2048]{1,0:T(8,128)}, f32[32,8,128]{2,1,0:T(8,128)}, /*index=5*/f32[8,512]{1,0:T(8,128)}) custom-call(f32[256,2048]{1,0:T(8,128)} %get-tuple-element.68.y2_ref, f32[256,2048]{1,0:T(8,128)} %get-tuple-element.69.ys_ref, ...), custom_call_target="tpu_custom_call" | custom-call | flops 2147483648 | bytes 14000000 | tf_op jit(solution)/shard_map/third_conv/pallas_call | solution.py:40
  191.6 7.9 %all-to-all-done.2.recv_ref = f32[32,8,128]{2,1,0:T(8,128)S(1)} async-done(((f32[32,8,128]{2,1,0:T(8,128)}), f32[32,8,128]{2,1,0:T(8,128)S(1)}, u32[]{:S(2)}, u32[]{:S(2)}) %all-to-all-start.2) | async-done | bytes 131104 | tf_op jit(solution)/shard_map/all_to_all | solution.py:737
  200.2 8.2 %fourth_conv.1 = (bf16[1024,256]{1,0:T(8,128)(2,1)}, bf16[1024,256]{1,0:T(8,128)(2,1)}, f32[256,2048]{1,0:T(8,128)}, f32[32,8,128]{2,1,0:T(8,128)}, f32[8,512]{1,0:T(8,128)}) custom-call(f32[256,2048]{1,0:T(8,128)} %get-tuple-element.72.y3_ref, f32[32,8,128]{2,1,0:T(8,128)} %copy-done.18, f32[2,5,512]{2,1,0:T(8,128)} %copy.86.norm_ref, ...), custom_call_target="tpu_custom_call" | custom-call | flops 2147483648 | bytes 10000000 | tf_op jit(solution)/shard_map/fourth_conv/pallas_call | solution.py:40
  213.7 5.9 %all-to-all-done.3.recv_ref = f32[32,8,128]{2,1,0:T(8,128)S(1)} async-done(((f32[32,8,128]{2,1,0:T(8,128)}), f32[32,8,128]{2,1,0:T(8,128)S(1)}, u32[]{:S(2)}, u32[]{:S(2)}) %all-to-all-start.3) | async-done | bytes 131104 | tf_op jit(solution)/shard_map/all_to_all | solution.py:737
  220.3 6.8 %heads.1 = (f32[256,512]{1,0:T(8,128)}, f32[256,128]{1,0:T(8,128)}, f32[256,2048]{1,0:T(8,128)}, f32[32,16,128]{2,1,0:T(8,128)}, f32[256,128]{1,0:T(8,128)}, /*index=5*/f32[8,512]{1,0:T(8,128)}) custom-call(f32[256,2048]{1,0:T(8,128)} %get-tuple-element.74.y4_ref, f32[256,2048]{1,0:T(8,128)} %get-tuple-element.75.h1_ref, f32[32,8,128]{2,1,0:T(8,128)} %copy-done.20, ...), custom_call_target="tpu_custom_call" | custom-call | flops 1000000000 | bytes 7000000 | tf_op jit(solution)/shard_map/heads/pallas_call | solution.py:40
  231.2 9.0 %all-to-all-done.4.recv_ref = f32[32,16,128]{2,1,0:T(8,128)S(1)} async-done(((f32[32,16,128]{2,1,0:T(8,128)}), f32[32,16,128]{2,1,0:T(8,128)S(1)}, u32[]{:S(2)}, u32[]{:S(2)}) %all-to-all-start.4) | async-done | bytes 262176 | tf_op jit(solution)/shard_map/all_to_all | solution.py:737
  240.9 6.3 %task_weights.1 = (f32[8,128]{1,0:T(8,128)}, f32[256,2048]{1,0:T(8,128)}, f32[32,16,128]{2,1,0:T(8,128)}) custom-call(f32[32,16,128]{2,1,0:T(8,128)} %copy-done.13, f32[40,128]{1,0:T(8,128)} %pad.8.square_ref, f32[256,128]{1,0:T(8,128)} %get-tuple-element.79.resid_ref, f32[128,512]{1,0:T(8,128)} %pad.9.turned_ref, f32[8,512]{1,0:T(8,128)} %get-tuple-element.71.base_ref, ...), custom_call_target="tpu_custom_call" | custom-call | flops 1000000000 | bytes 7000000 | tf_op jit(solution)/shard_map/task_weights/pallas_call | solution.py:40
  247.2 13.9 %all_to_all.46.recv_ref = f32[32,16,128]{2,1,0:T(8,128)} all-to-all(f32[32,16,128]{2,1,0:T(8,128)} %get-tuple-element.84), channel_id=1, replica_groups=mesh['batch'=8,'pass'=4] {'batch','pass'}, dimensions={0} | all-to-all | bytes 524288 | tf_op jit(solution)/shard_map/all_to_all | solution.py:737
  261.1 10.4 %fourth_back.1 = (bf16[256,2048]{1,0:T(8,128)(2,1)}, f32[256,2048]{1,0:T(8,128)}, f32[32,16,128]{2,1,0:T(8,128)}, f32[8,128]{1,0:T(8,128)}) custom-call(f32[256,2048]{1,0:T(8,128)} %get-tuple-element.83.u2_ref, f32[256,2048]{1,0:T(8,128)} %get-tuple-element.74.y4_ref, f32[32,16,128]{2,1,0:T(8,128)} %all_to_all.46.recv_ref, f32[2,5,512]{2,1,0:T(8,128)} %copy.86.norm_ref, ...), custom_call_target="tpu_custom_call" | custom-call | flops 2147483648 | bytes 14000000 | tf_op jit(solution)/shard_map/fourth_back/pallas_call | solution.py:40
  286.1 12.1 %third_back.1 = (bf16[256,2048]{1,0:T(8,128)(2,1)}, f32[256,2048]{1,0:T(8,128)}, f32[32,16,128]{2,1,0:T(8,128)}, f32[8,128]{1,0:T(8,128)}, f32[32,8,128]{2,1,0:T(8,128)}) custom-call(f32[256,2048]{1,0:T(8,128)} %get-tuple-element.86.u3_ref, f32[256,2048]{1,0:T(8,128)} %get-tuple-element.72.y3_ref, f32[32,16,128]{2,1,0:T(8,128)} %copy-done.10, ...), custom_call_target="tpu_custom_call" | custom-call | flops 2147483648 | bytes 18000000 | tf_op jit(solution)/shard_map/third_back/pallas_call | solution.py:40
  304.7 7.2 %all-to-all-done.7.recv_ref = f32[32,16,128]{2,1,0:T(8,128)S(1)} async-done(((f32[32,16,128]{2,1,0:T(8,128)}), f32[32,16,128]{2,1,0:T(8,128)S(1)}, u32[]{:S(2)}, u32[]{:S(2)}) %all-to-all-start.7) | async-done | bytes 262176 | tf_op jit(solution)/shard_map/all_to_all | solution.py:737
  312.6 11.4 %second_back.1 = (bf16[256,2048]{1,0:T(8,128)(2,1)}, bf16[256,2048]{1,0:T(8,128)(2,1)}, f32[256,2048]{1,0:T(8,128)}, f32[32,8,128]{2,1,0:T(8,128)}, f32[16,128]{1,0:T(8,128)}) custom-call(f32[256,2048]{1,0:T(8,128)} %get-tuple-element.89.u1_ref, f32[256,2048]{1,0:T(8,128)} %get-tuple-element.68.y2_ref, f32[256,2048]{1,0:T(8,128)} %get-tuple-element.69.ys_ref, ...), custom_call_target="tpu_custom_call" | custom-call | flops 2147483648 | bytes 18000000 | tf_op jit(solution)/shard_map/second_back/pallas_call | solution.py:40
  353.6 5.6 %collective-permute-done.23 = bf16[2,2,2,144,256]{4,3,2,1,0:T(8,128)(2,1)} collective-permute-done((bf16[2,2,2,144,256]{4,3,2,1,0:T(8,128)(2,1)}, bf16[2,2,2,144,256]{4,3,2,1,0:T(8,128)(2,1)}, u32[]{:S(2)}, u32[]{:S(2)}) %collective-permute-start.23) | collective-permute-done | bytes 589856 | tf_op jit(solution)/shard_map/ppermute | solution.py:741
  411.9 15.2 %collective-permute-done.26 = bf16[2,144,512]{2,1,0:T(8,128)(2,1)S(1)} collective-permute-done((bf16[2,144,512]{2,1,0:T(8,128)(2,1)S(1)}, bf16[2,144,512]{2,1,0:T(8,128)(2,1)S(1)}, u32[]{:S(2)}, u32[]{:S(2)}) %collective-permute-start.26) | collective-permute-done | bytes 294944 | tf_op jit(solution)/shard_map/ppermute | solution.py:741
  427.9 5.7 %input_grad.1 = f32[256,4096]{1,0:T(8,128)} custom-call(bf16[256,2048]{1,0:T(8,128)(2,1)} %get-tuple-element.93.dy_ref, bf16[256,2048]{1,0:T(8,128)(2,1)} %get-tuple-element.94.dys_ref, bf16[7168,512]{1,0:T(8,128)(2,1)} %all-gather.3.cloned.1.call-done.one_ref), custom_call_target="tpu_custom_call" | custom-call | flops 1946157056 | bytes 9000000 | tf_op jit(solution)/shard_map/input_grad/pallas_call | solution.py:40
  433.6 6.0 %reshape.211 = f32[256,4,4,256]{3,2,1,0:T(4,128)} reshape(f32[256,4096]{1,0:T(8,128)} %input_grad.1) | data formatting | bytes 8388608 | tf_op jit(solution)/shard_map/reshape | solution.py:1113
  448.7 8.2 %collective-permute-done.6 = bf16[4,2,112,256]{3,2,1,0:T(8,128)(2,1)S(1)} collective-permute-done((bf16[4,2,112,256]{3,2,1,0:T(8,128)(2,1)S(1)}, bf16[4,2,112,256]{3,2,1,0:T(8,128)(2,1)S(1)}, u32[]{:S(2)}, u32[]{:S(2)}) %collective-permute-start.6) | collective-permute-done | bytes 458784 | tf_op jit(solution)/shard_map/ppermute | solution.py:741
  470.3 10.3 %collective-permute-done.10 = bf16[2,112,512]{2,1,0:T(8,128)(2,1)S(1)} collective-permute-done((bf16[2,112,512]{2,1,0:T(8,128)(2,1)S(1)}, bf16[2,112,512]{2,1,0:T(8,128)(2,1)S(1)}, u32[]{:S(2)}, u32[]{:S(2)}) %collective-permute-start.10) | collective-permute-done | bytes 229408 | tf_op jit(solution)/shard_map/ppermute | solution.py:741
  (224 shorter events, 155.8 us)
Async XLA Ops:
  7.2 80.5 %all-gather.3.cloned.1.call-start = ((), (), s32[]{:S(2)}) async-start(), calls=%async_computation.9 | async-start | bytes 7569408 | tf_op jit(solution)/shard_map/all_gather | solution.py:828
  9.1 169.2 %all-gather.5.cloned.1.call-start = ((), (), s32[]{:S(2)}) async-start(), calls=%async_computation.10 | async-start | bytes 9732096 | tf_op jit(solution)/shard_map/all_gather | solution.py:829
  94.0 17.0 %all-to-all-start = ((f32[32,16,128]{2,1,0:T(8,128)}), f32[32,16,128]{2,1,0:T(8,128)S(1)}, u32[]{:S(2)}, u32[]{:S(2)}) async-start(f32[32,16,128]{2,1,0:T(8,128)} %get-tuple-element.66), calls=%async_computation | async-start | bytes 524288 | tf_op jit(solution)/shard_map/all_to_all | solution.py:737
  271.5 13.9 %all-to-all-start.6 = ((f32[32,16,128]{2,1,0:T(8,128)}), f32[32,16,128]{2,1,0:T(8,128)S(1)}, u32[]{:S(2)}, u32[]{:S(2)}) async-start(f32[32,16,128]{2,1,0:T(8,128)} %get-tuple-element.87), calls=%async_computation.6 | async-start | bytes 524288 | tf_op jit(solution)/shard_map/all_to_all | solution.py:737
  278.1 85.3 %collective-permute-start = (bf16[2048,256]{1,0:T(8,128)(2,1)}, bf16[2048,256]{1,0:T(8,128)(2,1)S(1)}, u32[]{:S(2)}, u32[]{:S(2)}) collective-permute-start(bf16[2048,256]{1,0:T(8,128)(2,1)} %get-tuple-element.98), channel_id=1, source_target_pairs={{0,1},{1,0},{2,3},{3,2},{4,5},{5,4},{6,7},{7,6},{8,9},{9,8},{10,11... | collective-permute-start | bytes 3145736 | tf_op jit(solution)/shard_map/ppermute | solution.py:741
  279.6 94.0 %collective-permute-start.2 = (bf16[1024,256]{1,0:T(8,128)(2,1)}, bf16[1024,256]{1,0:T(8,128)(2,1)}, u32[]{:S(2)}, u32[]{:S(2)}) collective-permute-start(bf16[1024,256]{1,0:T(8,128)(2,1)} %get-tuple-element.100), channel_id=1, source_target_pairs={{0,1},{1,0},{2,3},{3,2},{4,5},{5,4},{6,7},{7,6},{8,9},{9,8},{10,11... | collective-permute-start | bytes 1572872 | tf_op jit(solution)/shard_map/ppermute | solution.py:741
  280.5 63.0 %collective-permute-start.13 = (bf16[1024,256]{1,0:T(8,128)(2,1)}, bf16[1024,256]{1,0:T(8,128)(2,1)}, u32[]{:S(2)}, u32[]{:S(2)}) collective-permute-start(bf16[1024,256]{1,0:T(8,128)(2,1)} %get-tuple-element.103), channel_id=1, source_target_pairs={{0,1},{1,0},{2,3},{3,2},{4,5},{5,4},{6,7},{7,6},{8,9},{9,8},{10,11... | collective-permute-start | bytes 1572872 | tf_op jit(solution)/shard_map/ppermute | solution.py:741
  280.8 46.7 %collective-permute-start.19 = (bf16[1024,256]{1,0:T(8,128)(2,1)}, bf16[1024,256]{1,0:T(8,128)(2,1)}, u32[]{:S(2)}, u32[]{:S(2)}) collective-permute-start(bf16[1024,256]{1,0:T(8,128)(2,1)} %get-tuple-element.106), channel_id=1, source_target_pairs={{0,1},{1,0},{2,3},{3,2},{4,5},{5,4},{6,7},{7,6},{8,9},{9,8},{10,11... | collective-permute-start | bytes 1572872 | tf_op jit(solution)/shard_map/ppermute | solution.py:741
  282.3 45.3 %collective-permute-start.20 = (bf16[256,2048]{1,0:T(8,128)(2,1)S(1)}, bf16[256,2048]{1,0:T(8,128)(2,1)}, u32[]{:S(2)}, u32[]{:S(2)}) collective-permute-start(bf16[256,2048]{1,0:T(8,128)(2,1)S(1)} %copy-done.31), channel_id=1, source_target_pairs={{0,1},{1,0},{2,3},{3,2},{4,5},{5,4},{6,7},{7,6},{8,9},{9,8},{10,11... | collective-permute-start | bytes 3145736 | tf_op jit(solution)/shard_map/ppermute | solution.py:741
  327.5 17.7 %collective-permute-start.14 = (bf16[256,2048]{1,0:T(8,128)(2,1)}, bf16[256,2048]{1,0:T(8,128)(2,1)}, u32[]{:S(2)}, u32[]{:S(2)}) collective-permute-start(bf16[256,2048]{1,0:T(8,128)(2,1)} %get-tuple-element.104.dy_ref), channel_id=1, source_target_pairs={{0,1},{1,0},{2,3},{3,2},{4,5},{5,4},{6,7},{7,6},{8,9},{9,8},{10,11... | collective-permute-start | bytes 3145736 | tf_op jit(solution)/shard_map/ppermute | solution.py:741
  327.6 46.5 %collective-permute-start.3 = (bf16[256,2048]{1,0:T(8,128)(2,1)}, bf16[256,2048]{1,0:T(8,128)(2,1)}, u32[]{:S(2)}, u32[]{:S(2)}) collective-permute-start(bf16[256,2048]{1,0:T(8,128)(2,1)} %get-tuple-element.101.dy_ref), channel_id=1, source_target_pairs={{0,1},{1,0},{2,3},{3,2},{4,5},{5,4},{6,7},{7,6},{8,9},{9,8},{10,11... | collective-permute-start | bytes 3145736 | tf_op jit(solution)/shard_map/ppermute | solution.py:741
  343.5 15.7 %collective-permute-start.23 = (bf16[2,2,2,144,256]{4,3,2,1,0:T(8,128)(2,1)}, bf16[2,2,2,144,256]{4,3,2,1,0:T(8,128)(2,1)}, u32[]{:S(2)}, u32[]{:S(2)}) collective-permute-start(bf16[2,2,2,144,256]{4,3,2,1,0:T(8,128)(2,1)} %dynamic-slice_bitcast_fusion.1), channel_id=1, source_target_pairs={{0,4},{1,5},{2,6},{3,7},{4,0},{5,1},{6,2},{7,3},{8,12},{9,13},{10,... | collective-permute-start | bytes 1769480 | tf_op jit(solution)/shard_map/ppermute | solution.py:741
  345.2 15.4 %collective-permute-start.21 = (bf16[2,2,2,144,256]{4,3,2,0,1:T(8,128)(2,1)}, bf16[2,2,2,144,256]{4,3,2,0,1:T(8,128)(2,1)}, u32[]{:S(2)}, u32[]{:S(2)}) collective-permute-start(bf16[2,2,2,144,256]{4,3,2,0,1:T(8,128)(2,1)} %bitcast.157), channel_id=1, source_target_pairs={{0,2},{1,3},{2,0},{3,1},{4,6},{5,7},{6,4},{7,5},{8,10},{9,11},{10,... | collective-permute-start | bytes 1769480 | tf_op jit(solution)/shard_map/ppermute | solution.py:741
  359.2 14.9 %collective-permute-start.4 = (bf16[256,2048]{1,0:T(8,128)(2,1)S(1)}, bf16[256,2048]{1,0:T(8,128)(2,1)S(1)}, u32[]{:S(2)}, u32[]{:S(2)}) collective-permute-start(bf16[256,2048]{1,0:T(8,128)(2,1)S(1)} %copy-done.2), channel_id=1, source_target_pairs={{0,1},{1,0},{2,3},{3,2},{4,5},{5,4},{6,7},{7,6},{8,9},{9,8},{10,11... | collective-permute-start | bytes 3145736 | tf_op jit(solution)/shard_map/ppermute | solution.py:741
  370.0 15.3 %collective-permute-start.17 = (bf16[2,2,2,144,256]{4,3,2,0,1:T(8,128)(2,1)}, bf16[2,2,2,144,256]{4,3,2,0,1:T(8,128)(2,1)S(1)}, u32[]{:S(2)}, u32[]{:S(2)}) collective-permute-start(bf16[2,2,2,144,256]{4,3,2,0,1:T(8,128)(2,1)} %bitcast.158), channel_id=1, source_target_pairs={{0,4},{1,5},{2,6},{3,7},{4,0},{5,1},{6,2},{7,3},{8,12},{9,13},{10,... | collective-permute-start | bytes 1769480 | tf_op jit(solution)/shard_map/ppermute | solution.py:741
  372.8 19.9 %collective-permute-start.1 = (bf16[256,2048]{1,0:T(8,128)(2,1)S(1)}, bf16[256,2048]{1,0:T(8,128)(2,1)}, u32[]{:S(2)}, u32[]{:S(2)}) collective-permute-start(bf16[256,2048]{1,0:T(8,128)(2,1)S(1)} %copy-done.3), channel_id=1, source_target_pairs={{0,1},{1,0},{2,3},{3,2},{4,5},{5,4},{6,7},{7,6},{8,9},{9,8},{10,11... | collective-permute-start | bytes 3145736 | tf_op jit(solution)/shard_map/ppermute | solution.py:741
  373.6 16.4 %collective-permute-start.15 = (bf16[2,2,2,144,256]{4,3,2,0,1:T(8,128)(2,1)}, bf16[2,2,2,144,256]{4,3,2,0,1:T(8,128)(2,1)}, u32[]{:S(2)}, u32[]{:S(2)}) collective-permute-start(bf16[2,2,2,144,256]{4,3,2,0,1:T(8,128)(2,1)} %bitcast.159), channel_id=1, source_target_pairs={{0,2},{1,3},{2,0},{3,1},{4,6},{5,7},{6,4},{7,5},{8,10},{9,11},{10,... | collective-permute-start | bytes 1769480 | tf_op jit(solution)/shard_map/ppermute | solution.py:741
  403.3 23.8 %collective-permute-start.26 = (bf16[2,144,512]{2,1,0:T(8,128)(2,1)S(1)}, bf16[2,144,512]{2,1,0:T(8,128)(2,1)S(1)}, u32[]{:S(2)}, u32[]{:S(2)}) collective-permute-start(bf16[2,144,512]{2,1,0:T(8,128)(2,1)S(1)} %get-tuple-element.169), channel_id=1, source_target_pairs={{0,16},{1,17},{2,18},{3,19},{4,20},{5,21},{6,22},{7,23},{8,24},{9,... | collective-permute-start | bytes 884744 | tf_op jit(solution)/shard_map/ppermute | solution.py:741
  403.3 23.8 %collective-permute-start.25 = (bf16[2,144,512]{2,1,0:T(8,128)(2,1)S(1)}, bf16[2,144,512]{2,1,0:T(8,128)(2,1)S(1)}, u32[]{:S(2)}, u32[]{:S(2)}) collective-permute-start(bf16[2,144,512]{2,1,0:T(8,128)(2,1)S(1)} %get-tuple-element.167), channel_id=1, source_target_pairs={{0,8},{1,9},{2,10},{3,11},{4,12},{5,13},{6,14},{7,15},{8,0},{9,1},... | collective-permute-start | bytes 884744 | tf_op jit(solution)/shard_map/ppermute | solution.py:741
  406.1 36.3 %collective-permute-start.5 = (bf16[4,2,2,112,256]{4,3,2,0,1:T(8,128)(2,1)}, bf16[4,2,2,112,256]{4,3,2,0,1:T(8,128)(2,1)}, u32[]{:S(2)}, u32[]{:S(2)}) collective-permute-start(bf16[4,2,2,112,256]{4,3,2,0,1:T(8,128)(2,1)} %bitcast.156), channel_id=1, source_target_pairs={{0,2},{1,3},{2,0},{3,1},{4,6},{5,7},{6,4},{7,5},{8,10},{9,11},{10,... | collective-permute-start | bytes 2752520 | tf_op jit(solution)/shard_map/ppermute | solution.py:741
  407.7 37.8 %collective-permute-start.7 = (bf16[4,2,2,112,256]{4,3,2,1,0:T(8,128)(2,1)}, bf16[4,2,2,112,256]{4,3,2,1,0:T(8,128)(2,1)}, u32[]{:S(2)}, u32[]{:S(2)}) collective-permute-start(bf16[4,2,2,112,256]{4,3,2,1,0:T(8,128)(2,1)} %dynamic-slice_bitcast_fusion), channel_id=1, source_target_pairs={{0,4},{1,5},{2,6},{3,7},{4,0},{5,1},{6,2},{7,3},{8,12},{9,13},{10,... | collective-permute-start | bytes 2752520 | tf_op jit(solution)/shard_map/ppermute | solution.py:741
  427.9 14.3 %collective-permute-start.28 = (bf16[144,512]{1,0:T(8,128)(2,1)}, bf16[144,512]{1,0:T(8,128)(2,1)S(1)}, u32[]{:S(2)}, u32[]{:S(2)}) collective-permute-start(bf16[144,512]{1,0:T(8,128)(2,1)} %fusion.28), channel_id=1, source_target_pairs={{0,1},{1,0},{2,3},{3,2},{4,5},{5,4},{6,7},{7,6},{8,9},{9,8},{10,11... | collective-permute-start | bytes 442376 | tf_op jit(solution)/shard_map/ppermute | solution.py:741
  462.3 18.3 %collective-permute-start.10 = (bf16[2,112,512]{2,1,0:T(8,128)(2,1)S(1)}, bf16[2,112,512]{2,1,0:T(8,128)(2,1)S(1)}, u32[]{:S(2)}, u32[]{:S(2)}) collective-permute-start(bf16[2,112,512]{2,1,0:T(8,128)(2,1)S(1)} %get-tuple-element.177), channel_id=1, source_target_pairs={{0,16},{1,17},{2,18},{3,19},{4,20},{5,21},{6,22},{7,23},{8,24},{9,... | collective-permute-start | bytes 688136 | tf_op jit(solution)/shard_map/ppermute | solution.py:741
  462.3 18.3 %collective-permute-start.9 = (bf16[2,112,512]{2,1,0:T(8,128)(2,1)S(1)}, bf16[2,112,512]{2,1,0:T(8,128)(2,1)S(1)}, u32[]{:S(2)}, u32[]{:S(2)}) collective-permute-start(bf16[2,112,512]{2,1,0:T(8,128)(2,1)S(1)} %get-tuple-element.176), channel_id=1, source_target_pairs={{0,8},{1,9},{2,10},{3,11},{4,12},{5,13},{6,14},{7,15},{8,0},{9,1},... | collective-permute-start | bytes 688136 | tf_op jit(solution)/shard_map/ppermute | solution.py:741
  (47 other events, 445.2 us)
Sparse Core Ops, SparseCore 0:
  11.4 76.1 all-gather.2
  91.1 87.1 all-gather.4
